TPU v7x, 512 devices: a whole 4x4x16 slice. The times are simulated.
512 devices in a mesh: dp: 128 (over x, z, core), outer: 4 (over y).
Axes of the slice: x: 4, y: 4, z: 16, core: 2. Of those that a mesh axis runs over, the one named last changes fastest.
Arguments:
- replica_grads: bfloat16 [128, 4, 128, 4608], P('dp', 'outer'), may hold values from -12 to 12, as said below
- hadamard_signs: int32 [256], replicated, may hold values from -1 to 1, as said below
- master_rows: float32 [128, 4608], P('dp'), may hold values from -0.3 to 0.3
- first_moment: float32 [128, 4608], P('dp'), may hold values from -6 to 6
- second_moment: float32 [128, 4608], P('dp'), may hold values from 0.5 to 4
Outputs:
- new_master: float32 [128, 4608], P('dp')
- new_first: float32 [128, 4608], P('dp')
- new_second: float32 [128, 4608], P('dp')
- updated_rows: bfloat16 [128, 4608], replicated
Inputs may be any that keep to these rules, and one draw needn't show every extreme that they name: `hadamard_signs`: every entry is -1 or +1. `replica_grads`: every entry lies in the stated range on every mesh.
All inputs are finite; a program needn't handle non-finite values.
Results may differ from a plain program's by a relative error of at most 0.001.
Values may be sent and summed in bfloat16 or wider, within the bound.
A program may use at most 64 MiB of HBM per device.

v0:
```python
import jax
import jax.numpy as jnp
from jax import lax
from jax.sharding import PartitionSpec as P

HAD = 256
STEP = 1000


beta_one = 0.9
beta_two = 0.95
rate = 0.001
decay = 0.1
tiny_eps = 1e-08
clip_level = 1.5


def hadamard_table():
    indices = jnp.arange(HAD, dtype=jnp.int32)
    parity = jnp.zeros((HAD, HAD), jnp.int32)
    for bit_index in range(HAD.bit_length() - 1):
        column = jnp.bitwise_and(jnp.right_shift(indices, bit_index), 1)
        parity = parity + column[:, None] * column[None, :]
    return (1 - 2 * (parity % 2)).astype(jnp.float32)


def per_device(replica_grads, hadamard_signs, master_rows, first_moment, second_moment):
    rows_all = replica_grads.shape[2]
    width = replica_grads.shape[3]
    blocks = width // HAD
    owned_count = master_rows.shape[0]
    table = hadamard_table()
    local_rows = replica_grads.reshape(rows_all * blocks, HAD)
    signed = local_rows * hadamard_signs.astype(jnp.bfloat16)[None, :]
    rotated = (
        jnp.dot(signed, table.astype(jnp.bfloat16), preferred_element_type=jnp.float32) * 0.0625
    )
    meansq = jnp.mean(rotated * rotated, axis=1)
    block_peak = lax.pmax(meansq, ("dp", "outer"))
    scales = jnp.sqrt(block_peak + 1e-06)
    quantized = jnp.clip(rotated / scales[:, None], -clip_level, clip_level).astype(jnp.bfloat16)
    quantized = lax.optimization_barrier(quantized)
    terms = quantized.astype(jnp.float32).reshape(rows_all, width)
    combined = lax.psum(terms, "outer")
    owned_sum = lax.psum_scatter(combined, "dp", scatter_dimension=0, tiled=True)
    offset = lax.axis_index("dp") * (owned_count * blocks)
    owned_scales = lax.dynamic_slice_in_dim(scales, offset, owned_count * blocks, 0)
    decoded = owned_sum.reshape(owned_count * blocks, HAD) * owned_scales[:, None]
    gradient = jnp.dot(decoded, table, precision=lax.Precision.HIGHEST) * 0.0625
    gradient = (gradient * hadamard_signs.astype(jnp.float32)[None, :]).reshape(owned_count, width)
    new_first = beta_one * first_moment + (1.0 - beta_one) * gradient
    new_second = beta_two * second_moment + (1.0 - beta_two) * gradient * gradient
    first_fix = 1.0 - beta_one**STEP
    second_fix = 1.0 - beta_two**STEP
    update = (
        new_first / first_fix / (jnp.sqrt(new_second / second_fix) + tiny_eps) + decay * master_rows
    )
    new_master = master_rows - rate * update
    gathered = lax.all_gather(new_master.astype(jnp.bfloat16), "dp", axis=0, tiled=True)
    return (new_master, new_first, new_second, gathered)


def solution(mesh):
    in_specs = (P("dp", "outer", None, None), P(), P("dp", None), P("dp", None), P("dp", None))
    out_specs = (P("dp", None), P("dp", None), P("dp", None), P())
    return jax.shard_map(
        per_device, mesh=mesh, in_specs=in_specs, out_specs=out_specs, check_vma=False
    )
```

profile of v0, /device:TPU:1, one launch (start us, length us, event | category | flops | bytes accessed | tf_op | source)
XLA Modules:
  0.0 637.7 jit_solution(1437633215664754116)
XLA Ops:
  7.2 0.0 all-reduce.3.cloned.1.call-start
  7.3 0.6 shift-right-arithmetic_and_fusion.2
  7.8 0.6 shift-right-arithmetic_and_fusion
  8.4 1.3 convert_element_type.21
  9.7 2.5 reshape.143
  12.1 1.7 multiply_reduce_fusion
  13.9 111.2 %pmax.7 = f32[2304]{0:T(1024)S(1)} all-reduce(f32[2304]{0:T(1024)S(1)} %broadcast_multiply_fusion), channel_id=1, replica_groups=mesh['dp'=128,'outer'=4] {'dp','outer'}, use_global_device_ids=true, to_apply=%region_1.2 | all-reduce | flops 2304 | bytes 18432 | tf_op jit(solution)/shard_map/pmax | solution.py:39
  125.1 0.2 clamp_convert_fusion
  125.3 0.6 copy.11
  125.9 1.8 reshape.149
  127.7 0.0 copy-start.10
  127.7 0.0 copy-start.13
  127.8 0.0 all-reduce.3.cloned.1.call-update
  127.8 0.0 all-gather.3.cloned.1.call-start
  127.9 0.1 dynamic_slice.3
  128.0 1.3 dynamic-slice
  129.3 341.6 %all-reduce.3.cloned.1.call-done = f32[128,4608]{1,0:T(8,128)} async-done(((f32[128,4608]{1,0:T(8,128)}), f32[128,4608]{1,0:T(8,128)}) %all-reduce.3.cloned.1.call-update) | async-done | bytes 2359312
  470.9 1.6 constant_dynamic-slice_fusion
  472.4 13.2 %psum.8 = f32[1,4608]{1,0:T(1,128)S(1)} all-reduce(f32[1,4608]{1,0:T(1,128)S(1)} %constant_dynamic-slice_fusion), channel_id=1, replica_groups=mesh['dp'=128,'outer'=4] {'outer'}, use_global_device_ids=true, to_apply=%region_2.3 | all-reduce | flops 4608 | bytes 36864 | tf_op jit(solution)/shard_map/psum | solution.py:44
  485.8 0.6 fusion.1
  486.4 0.7 convert_bitcast_fusion
  487.2 0.0 all-gather.3.cloned.1.call-update
  487.2 140.9 %all-gather.3.cloned.1.call-done = bf16[128,1,4608]{2,1,0:T(2,128)(2,1)} async-done(((bf16[1,1,4608]{2,1,0:T(2,128)(2,1)}), bf16[128,1,4608]{2,1,0:T(2,128)(2,1)}) %all-gather.3.cloned.1.call-update) | async-done | bytes 1179664 | tf_op jit(solution)/shard_map/all_gather | solution.py:59
  628.0 2.8 copy.15
  (34 shorter events, 0.2 us)
Async XLA Ops:
  7.2 463.7 %all-reduce.3.cloned.1.call-start = ((), (), s32[]{:S(2)}) async-start(), calls=%async_computation.1 | async-start | bytes 4718592
  7.2 6.6 %copy-start.4 = (s32[256]{0:T(256)}, s32[256]{0:T(256)S(1)}, u32[]{:S(2)}) copy-start(s32[256]{0:T(256)S(1)} %get-tuple-element.17) | copy-start | bytes 3076
  7.2 6.6 %copy-start.6 = (s32[256]{0:T(256)}, s32[256]{0:T(256)S(1)}, u32[]{:S(2)}) copy-start(s32[256]{0:T(256)S(1)} %get-tuple-element.14) | copy-start | bytes 3076
  7.3 6.6 %copy-start.8 = (s32[256]{0:T(256)}, s32[256]{0:T(256)S(1)}, u32[]{:S(2)}) copy-start(s32[256]{0:T(256)S(1)} %get-tuple-element.15) | copy-start | bytes 3076
  127.7 1.6 copy-start.3
  127.7 358.0 %copy-start.5 = (s32[256]{0:T(256)S(1)}, s32[256]{0:T(256)}, u32[]{:S(2)}) copy-start(s32[256]{0:T(256)} %copy-done.4) | copy-start | bytes 3076
  127.7 358.0 %copy-start.7 = (s32[256]{0:T(256)S(1)}, s32[256]{0:T(256)}, u32[]{:S(2)}) copy-start(s32[256]{0:T(256)} %copy-done.6) | copy-start | bytes 3076
  127.7 358.0 %copy-start.9 = (s32[256]{0:T(256)S(1)}, s32[256]{0:T(256)}, u32[]{:S(2)}) copy-start(s32[256]{0:T(256)} %copy-done.8) | copy-start | bytes 3076
  127.7 358.0 %copy-start.10 = (s32[256]{0:T(256)S(1)}, s32[256]{0:T(256)}, u32[]{:S(2)}) copy-start(s32[256]{0:T(256)} %get-tuple-element.12) | copy-start | bytes 3076
  127.7 358.0 %copy-start.11 = (s32[256]{0:T(256)S(1)}, s32[256]{0:T(256)}, u32[]{:S(2)}) copy-start(s32[256]{0:T(256)} %get-tuple-element.13) | copy-start | bytes 3076
  127.7 358.0 %copy-start.12 = (s32[256]{0:T(256)S(1)}, s32[256]{0:T(256)}, u32[]{:S(2)}) copy-start(s32[256]{0:T(256)} %get-tuple-element.10) | copy-start | bytes 3076
  127.7 358.0 %copy-start.13 = (s32[256]{0:T(256)S(1)}, s32[256]{0:T(256)}, u32[]{:S(2)}) copy-start(s32[256]{0:T(256)} %get-tuple-element.11) | copy-start | bytes 3076
  127.7 358.6 %copy-start = (f32[1,4608]{1,0:T(1,128)S(1)}, f32[1,4608]{1,0:T(1,128)}, u32[]{:S(2)}) copy-start(f32[1,4608]{1,0:T(1,128)} %param.7) | copy-start | bytes 55300
  127.8 358.6 %copy-start.1 = (f32[1,4608]{1,0:T(1,128)S(1)}, f32[1,4608]{1,0:T(1,128)}, u32[]{:S(2)}) copy-start(f32[1,4608]{1,0:T(1,128)} %param.9) | copy-start | bytes 55300
  127.8 358.6 %copy-start.2 = (f32[1,4608]{1,0:T(1,128)S(1)}, f32[1,4608]{1,0:T(1,128)}, u32[]{:S(2)}) copy-start(f32[1,4608]{1,0:T(1,128)} %param.8) | copy-start | bytes 55300
  127.8 500.2 %all-gather.3.cloned.1.call-start = ((), (), s32[]{:S(2)}) async-start(), calls=%async_computation | async-start | bytes 2377728 | tf_op jit(solution)/shard_map/all_gather | solution.py:59
Sparse Core Ops, SparseCore 0:
  127.9 342.8 all-reduce.2
  487.3 140.6 all-gather.2
where the time goes:
time: 638 us
  waiting for transfers between devices  482 us (76%)
  blocking collectives  124 us (19%)
  between operations  14.3 us (2%)
  local copies, waits for them, and re-layouts  10.8 us (2%)
    unnamed x3, waiting for transfers between devices  342 us
    all_gather x1, waiting for transfers between devices, per_device(): lax.all_gather(new_master.astype(jnp.bfloat16), 'dp', axis=0, tiled=True)  141 us
    pmax x1, blocking collectives, per_device(): block_peak = lax.pmax(meansq, ('dp', 'outer'))  111 us
    psum x1, blocking collectives, per_device(): combined = lax.psum(terms, 'outer')  13.2 us
  transfers between devices with their start and end apart: 2, of which 2 were waited for; matrix products, arithmetic and copies ran while one was open for 0% of the time, Pallas kernels for 0%

commit v1 on v0

v1 whole, which is shorter than its diff:
```python
import functools

import jax
import jax.numpy as jnp
from jax import lax
from jax.experimental import pallas as pl
from jax.experimental.pallas import tpu as pltpu
from jax.sharding import PartitionSpec as P

HAD = 256
LANES = 128
STEP = 1000
CORES = 2

beta_one = 0.9
beta_two = 0.95
rate = 0.001
decay = 0.1
tiny_eps = 1e-08
clip_level = 1.5
first_fix = 1.0 - beta_one**STEP
second_fix = 1.0 - beta_two**STEP

FIXED = 8192.0

F32 = jnp.float32
BF16 = jnp.bfloat16
MESH = pl.DeviceIdType.MESH


def ring_distance(offset, size):
    return min(offset, size - offset)


def hadamard(dtype):
    bits = lax.broadcasted_iota(jnp.int32, (HAD, HAD), 0) & lax.broadcasted_iota(
        jnp.int32, (HAD, HAD), 1
    )
    bits = bits ^ (bits >> 4)
    bits = bits ^ (bits >> 2)
    bits = bits ^ (bits >> 1)
    return (1 - 2 * (bits & 1)).astype(F32).astype(dtype)


def split_three(value):
    high = value.astype(BF16)
    rest = value - high.astype(F32)
    middle = rest.astype(BF16)
    low = (rest - middle.astype(F32)).astype(BF16)
    return high, middle, low


def dot(a, b):
    return jnp.dot(a, b, preferred_element_type=F32)


def kernel(
    sizes,
    grads_hbm,
    signs_ref,
    master_ref,
    first_ref,
    second_ref,
    new_master_ref,
    new_first_ref,
    new_second_ref,
    out_ref,
    x_ref,
    rot_ref,
    had_ref,
    perm_ref,
    adam_ref,
    ms_ref,
    ra_ref,
    vb_ref,
    rb_ref,
    vc_ref,
    rc_ref,
    peak_ref,
    inv_ref,
    col_ref,
    qs_ref,
    qr_ref,
    s_ref,
    rxy_ref,
    zs_ref,
    rz_ref,
    tot_ref,
    agz_ref,
    gb_ref,
    load_sem,
    send_sems,
    recv_sems,
):
    NX, NY, NZ, NB, W = sizes
    rows = NX * NZ * CORES
    half = NX * NZ
    HB = NB // 2

    dp = lax.axis_index("dp")
    y = lax.axis_index("outer")
    c = lax.rem(dp, CORES)
    z = lax.rem(dp // CORES, NZ)
    x = dp // (CORES * NZ)

    def first_block(at):
        return (at * (NB - W) + NY - 2) // (NY - 1)

    def device(dx, dy, dz, dc):
        px = lax.rem(x + dx, NX)
        py = lax.rem(y + dy, NY)
        pz = lax.rem(z + dz, NZ)
        pc = lax.rem(c + dc, CORES)
        return ((px * NZ + pz) * CORES + pc, py)

    plane = [(ox, oy) for oy in range(NY) for ox in range(NX) if ox or oy]
    plane.sort(key=lambda o: -(ring_distance(o[0], NX) + ring_distance(o[1], NY)))
    line = sorted(range(1, NZ), key=lambda o: -ring_distance(o, NZ))
    column = sorted(range(1, NY), key=lambda o: -ring_distance(o, NY))
    core_peer = device(0, 0, 0, 1)
    plane_peer = {o: device(o[0], o[1], 0, 0) for o in plane}
    line_peer = {o: device(0, 0, o, 0) for o in line}

    barrier = pltpu.get_barrier_semaphore()
    peers = [line_peer[o] for o in line] + [plane_peer[o] for o in plane] + [core_peer]
    for peer in peers:
        pl.semaphore_signal(barrier, inc=1, device_id=peer, device_id_type=MESH)

    load = pltpu.make_async_copy(grads_hbm.at[0, 0], x_ref, load_sem)
    load.start()

    counter = [0]
    pending = []

    def copy(src, dst, peer, index):
        return pltpu.make_async_remote_copy(
            src_ref=src,
            dst_ref=dst,
            send_sem=send_sems.at[index],
            recv_sem=recv_sems.at[index],
            device_id=peer,
            device_id_type=MESH,
        )

    def take(count):
        base = counter[0]
        counter[0] += count
        return base

    def start(src, dst, peer, index):
        descriptor = copy(src, dst, peer, index)
        descriptor.start()
        pending.append(descriptor)
        return descriptor

    had_ref[...] = hadamard(BF16)
    p_at = lax.broadcasted_iota(jnp.int32, (rows, rows), 0)
    r_at = lax.broadcasted_iota(jnp.int32, (rows, rows), 1)
    r_core = r_at % CORES
    r_pair = r_at // CORES
    perm = (p_at == r_core * half + r_pair).astype(F32)
    perm_ref[...] = perm
    for at in range(NY):
        for k in range(W):
            lo = (first_block(at) + k) * HAD
            adam_ref[0, at, k : k + 1, :] = master_ref[0:1, lo : lo + HAD]
            adam_ref[1, at, k : k + 1, :] = first_ref[0:1, lo : lo + HAD]
            adam_ref[2, at, k : k + 1, :] = second_ref[0:1, lo : lo + HAD]

    load.wait()

    lane = lax.broadcasted_iota(jnp.int32, (HAD, LANES), 1)
    sums = jnp.zeros((rows, LANES), F32)
    for block in range(NB):
        value = x_ref[:, block * HAD : (block + 1) * HAD].astype(F32)
        square = value * value
        high = square.astype(BF16)
        low = (square - high.astype(F32)).astype(BF16)
        pick = (lane == block).astype(F32).astype(BF16)
        sums = sums + (dot(high, pick) + dot(low, pick))
    means = jnp.transpose(sums) * (1.0 / HAD)
    ms_ref[0] = means[0:HB, :]
    ms_ref[1] = means[HB:NB, :]

    pl.semaphore_wait(barrier, len(peers))

    base = take(1)
    stage = start(ms_ref.at[1 - c], ra_ref, core_peer, base)
    stage.wait_recv()
    peak = jnp.maximum(ms_ref[c], ra_ref[...])
    vb_ref[...] = peak

    base = take(len(plane))
    stages = [
        start(vb_ref, rb_ref.at[j], plane_peer[o], base + j) for j, o in enumerate(plane)
    ]
    for j, stage in enumerate(stages):
        stage.wait_recv()
        peak = jnp.maximum(peak, rb_ref[j])
    vc_ref[...] = peak

    base = take(len(line))
    stages = [start(vc_ref, rc_ref.at[j], line_peer[o], base + j) for j, o in enumerate(line)]

    table = had_ref[...]
    order = perm.astype(BF16)
    signs = signs_ref[...].astype(F32).astype(BF16)
    for block in range(NB):
        cols = slice(block * HAD, (block + 1) * HAD)
        sorted_rows = dot(order, x_ref[:, cols]).astype(BF16)
        rotated = dot(sorted_rows * signs, table) * 0.0625
        rot_ref[0, :, cols] = rotated[0:half]
        rot_ref[1, :, cols] = rotated[half:rows]

    for j, stage in enumerate(stages):
        stage.wait_recv()
        peak = jnp.maximum(peak, rc_ref[j])
    peak_ref[c] = peak
    base = take(1)
    start(peak_ref.at[c], peak_ref.at[c], core_peer, base)
    copy(peak_ref.at[1 - c], peak_ref.at[1 - c], core_peer, base).wait_recv()

    scale_low = jnp.sqrt(peak_ref[0] + 1e-06)
    scale_high = jnp.sqrt(peak_ref[1] + 1e-06)
    scales = jnp.concatenate([scale_low, scale_high], axis=0)
    inv_ref[...] = jnp.zeros_like(inv_ref)
    inv_ref[0:NB, :] = 1.0 / scales
    inverse = lax.dot_general(
        perm_ref[...],
        inv_ref[...],
        (((1,), (1,)), ((), ())),
        precision=lax.Precision.HIGHEST,
        preferred_element_type=F32,
    )

    orders = [oy for oy in column] + [0]
    core_base = take(NY)
    plane_base = take(len(plane))

    def quantize(which, at):
        begin = first_block(at)
        cols = pl.ds(pl.multiple_of(begin * HAD, HAD), W * HAD)
        factors = pltpu.roll(inverse, lax.rem(LANES - begin, LANES), 1)
        value = rot_ref[which, :, cols]
        picked = jnp.where(which == 0, factors[0:half], factors[half:rows])
        return jnp.concatenate(
            [
                jnp.clip(
                    value[:, k * HAD : (k + 1) * HAD] * picked[:, k : k + 1],
                    -clip_level,
                    clip_level,
                ).astype(BF16)
                for k in range(W)
            ],
            axis=1,
        )

    core_stages = []
    for i, oy in enumerate(orders):
        at = lax.rem(y + oy, NY)
        qs_ref[i] = quantize(1 - c, at)
        core_stages.append(start(qs_ref.at[i], qr_ref.at[i], core_peer, core_base + i))

    plane_stages = {}
    for i, oy in enumerate(orders):
        at = lax.rem(y + oy, NY)
        own = quantize(c, at).astype(F32)
        core_stages[i].wait_recv()
        both = (own + qr_ref[i].astype(F32)) * FIXED
        coded = jnp.round(both).astype(jnp.int32).astype(jnp.int16)
        for px in range(NX):
            s_ref[i, px] = coded[px * NZ : (px + 1) * NZ]
        for j, o in enumerate(plane):
            if o[1] == oy:
                plane_stages[j] = start(
                    s_ref.at[i, lax.rem(x + o[0], NX)],
                    rxy_ref.at[j],
                    plane_peer[o],
                    plane_base + j,
                )

    row_lane = lax.broadcasted_iota(jnp.int32, (NB, rows), 1)
    own_scale = jnp.sum(jnp.where(row_lane == dp, scales, 0.0), axis=1, keepdims=True)
    own_scale = jnp.broadcast_to(own_scale, (NB, HAD))
    for at in range(NY):
        col_ref[at] = own_scale[first_block(at) : first_block(at) + W]

    total = s_ref[NY - 1, x].astype(jnp.int32)
    for j in sorted(plane_stages, key=lambda j: -j):
        plane_stages[j].wait_recv()
        total = total + rxy_ref[j].astype(jnp.int32)
    for k in range(W):
        for h in range(2):
            lo = k * HAD + h * LANES
            zs_ref[:, h * W + k, :] = total[:, lo : lo + LANES]

    base = take(len(line))
    stages = [
        start(zs_ref.at[lax.rem(z + o, NZ)], rz_ref.at[j], line_peer[o], base + j)
        for j, o in enumerate(line)
    ]
    total = zs_ref[z]
    for j in reversed(range(len(line))):
        stages[j].wait_recv()
        total = total + rz_ref[j]
    tot_ref[y] = total

    sign_row = signs_ref[...].astype(F32)

    def adam(summed, scale, master, first, second):
        parts = split_three(summed * scale)
        gradient = (dot(parts[0], table) + dot(parts[1], table)) + dot(parts[2], table)
        gradient = gradient * 0.0625 * sign_row
        new_first = beta_one * first + (1.0 - beta_one) * gradient
        new_second = beta_two * second + (1.0 - beta_two) * gradient * gradient
        update = (
            new_first * (1.0 / first_fix) / (jnp.sqrt(new_second * (1.0 / second_fix)) + tiny_eps)
            + decay * master
        )
        return master - rate * update, new_first, new_second

    def wide(value):
        value = value.astype(F32) * (1.0 / FIXED)
        return jnp.concatenate([value[0:W], value[W : 2 * W]], axis=1)

    updated, _, _ = adam(
        wide(total), col_ref[y], adam_ref[0, y], adam_ref[1, y], adam_ref[2, y]
    )
    updated = updated.astype(BF16).astype(F32)
    agz_ref[z, 0:W] = updated[:, 0:LANES]
    agz_ref[z, W : 2 * W] = updated[:, LANES:HAD]

    line_base = take(len(line))
    for j, o in enumerate(line):
        start(agz_ref.at[z], agz_ref.at[z], line_peer[o], line_base + j)
    column_base = take(len(column))
    for j, o in enumerate(column):
        start(tot_ref.at[y], tot_ref.at[y], plane_peer[(0, o)], column_base + j)

    for j, o in enumerate(column):
        source = lax.rem(y + NY - o, NY)
        copy(
            tot_ref.at[source], tot_ref.at[source], plane_peer[(0, o)], column_base + j
        ).wait_recv()
    for at in range(NY):
        results = adam(
            wide(tot_ref[at]), col_ref[at], adam_ref[0, at], adam_ref[1, at], adam_ref[2, at]
        )
        for ref, value in zip((new_master_ref, new_first_ref, new_second_ref), results):
            for k in range(W):
                lo = (first_block(at) + k) * HAD
                ref[0:1, lo : lo + HAD] = value[k : k + 1, :]

    for j, o in reversed(list(enumerate(line))):
        source = lax.rem(z + NZ - o, NZ)
        copy(agz_ref.at[source], agz_ref.at[source], line_peer[o], line_base + j).wait_recv()
    for k in range(W):
        for h in range(2):
            lo = k * HAD + h * LANES
            gb_ref[c, y, x, :, lo : lo + LANES] = agz_ref[:, h * W + k, :].astype(BF16)

    plane_base = take(len(plane))
    core_base = take(len(plane) + 1)
    for j, o in enumerate(plane):
        start(gb_ref.at[c, y, x], gb_ref.at[c, y, x], plane_peer[o], plane_base + j)
    start(gb_ref.at[c, y, x], gb_ref.at[c, y, x], core_peer, core_base + len(plane))
    for j, o in reversed(list(enumerate(plane))):
        sx = lax.rem(x + NX - o[0], NX)
        sy = lax.rem(y + NY - o[1], NY)
        here = gb_ref.at[c, sy, sx]
        copy(here, here, plane_peer[o], plane_base + j).wait_recv()
        start(here, here, core_peer, core_base + j)
    for j, o in list(enumerate(plane)) + [(len(plane), (0, 0))]:
        sx = lax.rem(x + NX - o[0], NX)
        sy = lax.rem(y + NY - o[1], NY)
        there = gb_ref.at[1 - c, sy, sx]
        copy(there, there, core_peer, core_base + j).wait_recv()

    back = jnp.transpose(perm_ref[...]).astype(BF16)
    done = 0
    for at in range(NY):
        skip = done - first_block(at)
        for k in range(skip, W):
            cols = slice(k * HAD, (k + 1) * HAD)
            block = jnp.concatenate(
                [
                    gb_ref[0, at, :, :, cols].reshape(half, HAD),
                    gb_ref[1, at, :, :, cols].reshape(half, HAD),
                ],
                axis=0,
            )
            lo = (first_block(at) + k) * HAD
            out_ref[:, lo : lo + HAD] = dot(back, block).astype(BF16)
        done = first_block(at) + W

    for descriptor in pending:
        descriptor.wait_send()


def build(mesh, NX, NZ, NB):
    NY = mesh.shape["outer"]
    W = -(-NB // NY)
    sizes = (NX, NY, NZ, NB, W)
    rows = NX * NZ * CORES
    half = NX * NZ
    HB = NB // 2
    n_plane = NX * NY - 1
    n_line = NZ - 1
    messages = 1 + n_plane + n_line + 1 + NY + n_plane + n_line
    messages += n_line + (NY - 1) + n_plane + n_plane + 1
    width = NB * HAD
    scratch = [
        pltpu.VMEM((rows, width), BF16),
        pltpu.VMEM((2, half, width), F32),
        pltpu.VMEM((HAD, HAD), BF16),
        pltpu.VMEM((rows, rows), F32),
        pltpu.VMEM((3, NY, W, HAD), F32),
        pltpu.VMEM((2, HB, rows), F32),
        pltpu.VMEM((HB, rows), F32),
        pltpu.VMEM((HB, rows), F32),
        pltpu.VMEM((n_plane, HB, rows), F32),
        pltpu.VMEM((HB, rows), F32),
        pltpu.VMEM((n_line, HB, rows), F32),
        pltpu.VMEM((2, HB, rows), F32),
        pltpu.VMEM((LANES, rows), F32),
        pltpu.VMEM((NY, W, HAD), F32),
        pltpu.VMEM((NY, half, W * HAD), BF16),
        pltpu.VMEM((NY, half, W * HAD), BF16),
        pltpu.VMEM((NY, NX, NZ, W * HAD), jnp.int16),
        pltpu.VMEM((n_plane, NZ, W * HAD), jnp.int16),
        pltpu.VMEM((NZ, 2 * W, LANES), jnp.int32),
        pltpu.VMEM((n_line, 2 * W, LANES), jnp.int32),
        pltpu.VMEM((NY, 2 * W, LANES), jnp.int32),
        pltpu.VMEM((NZ, 2 * W, LANES), F32),
        pltpu.VMEM((2, NY, NX, NZ, W * HAD), BF16),
        pltpu.SemaphoreType.DMA,
        pltpu.SemaphoreType.DMA((messages,)),
        pltpu.SemaphoreType.DMA((messages,)),
    ]
    vmem = pl.BlockSpec(memory_space=pltpu.VMEM)
    row = jax.ShapeDtypeStruct((1, width), F32)

    def per_device(replica_grads, hadamard_signs, master_rows, first_moment, second_moment):
        return pl.pallas_call(
            functools.partial(kernel, sizes),
            out_shape=(row, row, row, jax.ShapeDtypeStruct((rows, width), BF16)),
            in_specs=[pl.BlockSpec(memory_space=pl.ANY)] + [vmem] * 4,
            out_specs=(vmem, vmem, vmem, vmem),
            scratch_shapes=scratch,
            compiler_params=pltpu.CompilerParams(
                collective_id=0, has_side_effects=True, vmem_limit_bytes=56 * 2**20
            ),
        )(
            replica_grads,
            hadamard_signs.reshape(1, HAD),
            master_rows,
            first_moment,
            second_moment,
        )

    in_specs = (P("dp", "outer", None, None), P(), P("dp", None), P("dp", None), P("dp", None))
    out_specs = (P("dp", None), P("dp", None), P("dp", None), P())
    return jax.shard_map(
        per_device, mesh=mesh, in_specs=in_specs, out_specs=out_specs, check_vma=False
    )


def solution(mesh):
    return build(mesh, 4, 16, 18)
```

time: 638 us -> 76.8 us (0.12)
  waiting for transfers between devices: 482 us -> 0 us
  blocking collectives: 124 us -> 0 us
  Pallas kernels: 0 us -> 69.4 us
  between operations: 14.3 us -> 0.64 us
    unnamed x3 -> x0, waiting for transfers between devices: 342 us -> none
    all_gather x1 -> x0, waiting for transfers between devices: 141 us -> none  [per_device(): lax.all_gather(new_master.astype(jnp.bfloat16), 'dp', axis=0, tiled=True)]
    pmax x1 -> x0, blocking collectives: 111 us -> none  [per_device(): block_peak = lax.pmax(meansq, ('dp', 'outer'))]
    pallas_call x0 -> x1, Pallas kernels: none -> 69.4 us  [per_device(): pl.pallas_call(functools.partial(kernel, sizes), out_shape=(row, row, row...]
    psum x1 -> x0, blocking collectives: 13.2 us -> none  [per_device(): combined = lax.psum(terms, 'outer')]
  transfers between devices with their start and end apart: 2 -> 0, of which waited for: 2 -> 0; matrix products, arithmetic and copies ran while one was open for 0% -> 0% of each run, Pallas kernels for 0% -> 0%
where the time goes in v1:
time: 76.8 us; the launch traced here: 76.3 us
  Pallas kernels  69.4 us (90%)
  local copies, waits for them, and re-layouts  6.35 us (8%)
    pallas_call x1, Pallas kernels, per_device(): pl.pallas_call(functools.partial(kernel, sizes), out_shape=(row, row, row...  69.4 us
    unnamed x4, local copies, waits for them, and re-layouts  6.35 us

profile of v1, /device:TPU:1, one launch (start us, length us, event | category | flops | bytes accessed | tf_op | source)
XLA Modules:
  0.0 76.3 jit_solution(16625684067559695560)
XLA Ops:
  0.6 69.4 %shard_map.84 = (f32[1,4608]{1,0:T(1,128)}, f32[1,4608]{1,0:T(1,128)}, f32[1,4608]{1,0:T(1,128)}, bf16[128,4608]{1,0:T(8,128)(2,1)}) custom-call(bf16[1,1,128,4608]{3,2,1,0:T(8,128)(2,1)} %grads_hbm.1, s32[1,256]{1,0:T(1,128)} %bitcast.1, f32[1,4608]{1,0:T(1,128)} %master_ref.1, f32[1,4608]{1,0:T(1,128)} %first_ref.1, f32[1,4608]{1,0:T(1,128)} %second_ref.1), custom_call_target="tpu_custom_call" | custom-call | tf_op jit(solution)/shard_map/pallas_call | solution.py:444
  70.0 1.3 %copy.13 = f32[1,4608]{1,0:T(1,128)} copy(f32[1,4608]{1,0:T(1,128)} %get-tuple-element.8) | data formatting | bytes 36864
  71.3 1.3 %copy.14 = f32[1,4608]{1,0:T(1,128)} copy(f32[1,4608]{1,0:T(1,128)} %get-tuple-element.9) | data formatting | bytes 36864
  72.7 1.3 %copy.15 = f32[1,4608]{1,0:T(1,128)} copy(f32[1,4608]{1,0:T(1,128)} %get-tuple-element.10) | data formatting | bytes 36864
  74.0 2.4 %copy.16 = bf16[128,4608]{1,0:T(8,128)(2,1)} copy(bf16[128,4608]{1,0:T(8,128)(2,1)} %get-tuple-element.11) | data formatting | bytes 2359296

commit v2 on v0

v2 whole, which is shorter than its diff:
```python
import functools

import jax
import jax.numpy as jnp
from jax import lax
from jax.experimental import pallas as pl
from jax.experimental.pallas import tpu as pltpu
from jax.sharding import PartitionSpec as P

HAD = 256
LANES = 128
STEP = 1000
CORES = 2

beta_one = 0.9
beta_two = 0.95
rate = 0.001
decay = 0.1
tiny_eps = 1e-08
clip_level = 1.5
first_fix = 1.0 - beta_one**STEP
second_fix = 1.0 - beta_two**STEP

F32 = jnp.float32
BF16 = jnp.bfloat16
MESH = pl.DeviceIdType.MESH


def ring_distance(offset, size):
    return min(offset, size - offset)


def hadamard(dtype):
    bits = lax.broadcasted_iota(jnp.int32, (HAD, HAD), 0) & lax.broadcasted_iota(
        jnp.int32, (HAD, HAD), 1
    )
    bits = bits ^ (bits >> 4)
    bits = bits ^ (bits >> 2)
    bits = bits ^ (bits >> 1)
    return (1 - 2 * (bits & 1)).astype(F32).astype(dtype)


def split_three(value):
    high = value.astype(BF16)
    rest = value - high.astype(F32)
    middle = rest.astype(BF16)
    low = (rest - middle.astype(F32)).astype(BF16)
    return high, middle, low


def dot(a, b):
    return jnp.dot(a, b, preferred_element_type=F32)


def adam(gradient, master, first, second):
    new_first = beta_one * first + (1.0 - beta_one) * gradient
    new_second = beta_two * second + (1.0 - beta_two) * gradient * gradient
    update = (
        new_first * (1.0 / first_fix) / (jnp.sqrt(new_second * (1.0 / second_fix)) + tiny_eps)
        + decay * master
    )
    return master - rate * update, new_first, new_second


def piece_start(sizes, at):
    NX, NY, NZ, NB, W = sizes
    return (at * (NB - W) + NY - 2) // (NY - 1)


def exchange_kernel(
    sizes,
    grads_hbm,
    signs_ref,
    master_ref,
    first_ref,
    second_ref,
    gb_ref,
    grad_ref,
    x_ref,
    table_ref,
    signed_ref,
    adam_ref,
    bulk_ref,
    rbulk_ref,
    rot_ref,
    m1_ref,
    r1_ref,
    m2_ref,
    r2_ref,
    m3_ref,
    r3_ref,
    acc_ref,
    racc_ref,
    zs_ref,
    rz_ref,
    agz_ref,
    load_sem,
    send_sems,
    recv_sems,
):
    NX, NY, NZ, NB, W = sizes
    rows = NX * NZ * CORES
    pair = CORES * NZ
    stride = LANES // NZ

    dp = lax.axis_index("dp")
    y = lax.axis_index("outer")
    c = lax.rem(dp, CORES)
    z = lax.rem(dp // CORES, NZ)
    x = dp // (CORES * NZ)

    def first_block(at):
        return piece_start(sizes, at)

    def device(dx, dy, dz, dc):
        px = lax.rem(x + dx, NX)
        py = lax.rem(y + dy, NY)
        pz = lax.rem(z + dz, NZ)
        pc = lax.rem(c + dc, CORES)
        return ((px * NZ + pz) * CORES + pc, py)

    def hops(o):
        return ring_distance(o[0], NX) + ring_distance(o[1], NY)

    plane = [(ox, oy) for oy in range(NY) for ox in range(NX) if ox or oy]
    plane.sort(key=lambda o: -hops(o))
    line = sorted(range(1, NZ), key=lambda o: -ring_distance(o, NZ))
    column = sorted(range(1, NY), key=lambda o: -ring_distance(o, NY))
    core_peer = device(0, 0, 0, 1)
    plane_peer = [device(o[0], o[1], 0, 0) for o in plane]
    line_peer = [device(0, 0, o, 0) for o in line]
    here = len(plane)

    barrier = pltpu.get_barrier_semaphore()
    peers = line_peer + plane_peer + [core_peer]
    for peer in peers:
        pl.semaphore_signal(barrier, inc=1, device_id=peer, device_id_type=MESH)

    load = pltpu.make_async_copy(grads_hbm.at[0, 0], x_ref, load_sem)
    load.start()

    counter = [0]
    pending = []

    def copy(src, dst, peer, index):
        return pltpu.make_async_remote_copy(
            src_ref=src,
            dst_ref=dst,
            send_sem=send_sems.at[index],
            recv_sem=recv_sems.at[index],
            device_id=peer,
            device_id_type=MESH,
        )

    def take(count):
        base = counter[0]
        counter[0] += count
        return base

    def start(src, dst, peer, index):
        descriptor = copy(src, dst, peer, index)
        descriptor.start()
        pending.append(descriptor)
        return descriptor

    p_at = lax.broadcasted_iota(jnp.int32, (rows, rows), 0)
    r_at = lax.broadcasted_iota(jnp.int32, (rows, rows), 1)
    r_core = r_at % CORES
    r_z = (r_at // CORES) % NZ
    r_x = r_at // pair
    order = (p_at == r_x * pair + r_core * NZ + r_z).astype(F32).astype(BF16)

    table = hadamard(BF16)
    table_ref[...] = table

    load.wait()

    lane = lax.broadcasted_iota(jnp.int32, (HAD, LANES), 1)
    picks = [(lane % stride == k).astype(F32).astype(BF16) for k in range(W)]
    sums = [jnp.zeros((rows, LANES), F32) for _ in range(NY)]
    for block in range(NB):
        value = dot(order, x_ref[:, block * HAD : (block + 1) * HAD])
        square = value * value
        high = square.astype(BF16)
        low = (square - high.astype(F32)).astype(BF16)
        both = jnp.concatenate([high, low], axis=0)
        value = value.astype(BF16).reshape(NX, pair, HAD)
        for at in range(NY):
            k = block - first_block(at)
            if 0 <= k < W:
                part = dot(both, picks[k])
                sums[at] = sums[at] + (part[0:rows] + part[rows : 2 * rows])
                bulk_ref[at, :, :, k * HAD : (k + 1) * HAD] = value
    row_at = lax.broadcasted_iota(jnp.int32, (rows, LANES), 0)
    lane_at = lax.broadcasted_iota(jnp.int32, (rows, LANES), 1)
    mine = row_at % NZ == lane_at // stride
    for at in range(NY):
        packed = jnp.where(mine, sums[at], 0.0).reshape(NX * CORES, NZ, LANES)
        packed = jnp.sum(packed, axis=1) * (1.0 / HAD)
        for px in range(NX):
            m1_ref[at, px] = packed[px * CORES : (px + 1) * CORES]

    pl.semaphore_wait(barrier, len(peers))

    base = take(here)
    stages = []
    for j, o in enumerate(plane):
        piece = m1_ref.at[lax.rem(y + o[1], NY), lax.rem(x + o[0], NX)]
        stages.append(start(piece, r1_ref.at[j], plane_peer[j], base + j))
    base = take(here)
    bulk_stages = []
    for j, o in enumerate(plane):
        piece = bulk_ref.at[lax.rem(y + o[1], NY), lax.rem(x + o[0], NX)]
        bulk_stages.append(start(piece, rbulk_ref.at[j], plane_peer[j], base + j))
    rbulk_ref[here] = bulk_ref[y, x]

    diagonal = lax.broadcasted_iota(jnp.int32, (HAD, HAD), 0) == lax.broadcasted_iota(
        jnp.int32, (HAD, HAD), 1
    )
    sign_row = signs_ref[...].astype(F32)
    signed_ref[...] = dot(
        jnp.where(diagonal, sign_row, 0.0).astype(BF16), table
    ).astype(BF16)
    for at in range(NY):
        for k in range(W):
            lo = (first_block(at) + k) * HAD
            adam_ref[0, at, k : k + 1, :] = master_ref[0:1, lo : lo + HAD]
            adam_ref[1, at, k : k + 1, :] = first_ref[0:1, lo : lo + HAD]
            adam_ref[2, at, k : k + 1, :] = second_ref[0:1, lo : lo + HAD]

    peak = m1_ref[y, x]
    for j in reversed(range(here)):
        stages[j].wait_recv()
        peak = jnp.maximum(peak, r1_ref[j])
    m2_ref[...] = peak
    base = take(1)
    start(m2_ref, r2_ref, core_peer, base).wait_recv()
    peak = jnp.maximum(peak, r2_ref[...])
    m3_ref[...] = peak
    base = take(len(line))
    stages = [start(m3_ref, r3_ref.at[j], line_peer[j], base + j) for j in range(len(line))]

    signed = signed_ref[...]
    far = len([o for o in plane if hops(o) > 2])
    for lo_slot, hi_slot in ((far, here + 1), (0, far)):
        count = hi_slot - lo_slot
        if count == 0:
            continue
        for j in reversed(range(lo_slot, min(hi_slot, here))):
            bulk_stages[j].wait_recv()
        for k in range(W):
            cols = slice(k * HAD, (k + 1) * HAD)
            value = rbulk_ref[lo_slot:hi_slot, :, cols].reshape(count * pair, HAD)
            rot_ref[lo_slot:hi_slot, :, cols] = dot(value, signed).reshape(count, pair, HAD)

    for j in reversed(range(len(line))):
        stages[j].wait_recv()
        peak = jnp.maximum(peak, r3_ref[j])

    scales = jnp.sqrt(peak + 1e-06)
    inverse = 0.0625 / scales
    z_at = lax.broadcasted_iota(jnp.int32, (NZ, LANES), 0)
    l_at = lax.broadcasted_iota(jnp.int32, (NZ, LANES), 1)
    base = take(W)
    core_stages = []
    for k in range(W):
        cols = slice(k * HAD, (k + 1) * HAD)
        pick = l_at == z_at * stride + k
        factor = jnp.concatenate(
            [
                jnp.sum(
                    jnp.where(pick, jnp.broadcast_to(inverse[g : g + 1], (NZ, LANES)), 0.0),
                    axis=1,
                    keepdims=True,
                )
                for g in range(CORES)
            ],
            axis=0,
        )
        factor = jnp.broadcast_to(factor, (pair, HAD))
        total = jnp.zeros((pair, HAD), F32)
        for j in range(here + 1):
            value = jnp.clip(rot_ref[j, :, cols] * factor, -clip_level, clip_level)
            total = total + value.astype(BF16).astype(F32)
        acc_ref[0, :, cols] = total[0:NZ]
        acc_ref[1, :, cols] = total[NZ:pair]
        core_stages.append(
            start(acc_ref.at[1 - c, :, cols], racc_ref.at[:, cols], core_peer, base + k)
        )

    w_at = lax.broadcasted_iota(jnp.int32, (W, LANES), 0)
    k_at = lax.broadcasted_iota(jnp.int32, (W, LANES), 1)
    own = jnp.broadcast_to(jnp.where(c == 0, scales[0:1], scales[1:2]), (W, LANES))
    own_scale = jnp.sum(
        jnp.where(k_at == z * stride + w_at, own, 0.0), axis=1, keepdims=True
    )

    for k in range(W):
        core_stages[k].wait_recv()
        for h in range(2):
            cols = slice(k * HAD + h * LANES, k * HAD + (h + 1) * LANES)
            zs_ref[:, h * W + k, :] = acc_ref[c, :, cols] + racc_ref[:, cols]

    base = take(len(line))
    stages = [
        start(zs_ref.at[lax.rem(z + o, NZ)], rz_ref.at[j], line_peer[j], base + j)
        for j, o in enumerate(line)
    ]
    total = zs_ref[z]
    for j in reversed(range(len(line))):
        stages[j].wait_recv()
        total = total + rz_ref[j]

    wide = jnp.concatenate([total[0:W], total[W : 2 * W]], axis=1)
    parts = split_three(wide * own_scale)
    table = table_ref[...]
    gradient = (dot(parts[0], table) + dot(parts[1], table)) + dot(parts[2], table)
    gradient = gradient * 0.0625 * sign_row
    grad_ref[y] = gradient
    updated, _, _ = adam(gradient, adam_ref[0, y], adam_ref[1, y], adam_ref[2, y])
    updated = updated.astype(BF16).astype(F32)
    agz_ref[z, 0:W] = updated[:, 0:LANES]
    agz_ref[z, W : 2 * W] = updated[:, LANES:HAD]

    base = take(len(line))
    for j in range(len(line)):
        start(agz_ref.at[z], agz_ref.at[z], line_peer[j], base + j)
    column_base = take(len(column))
    for j, o in enumerate(column):
        start(grad_ref.at[y], grad_ref.at[y], device(0, o, 0, 0), column_base + j)
    for j in reversed(range(len(line))):
        source = agz_ref.at[lax.rem(z + NZ - line[j], NZ)]
        copy(source, source, line_peer[j], base + j).wait_recv()
    for k in range(W):
        for h in range(2):
            lo = k * HAD + h * LANES
            gb_ref[c, y, x, :, lo : lo + LANES] = agz_ref[:, h * W + k, :].astype(BF16)

    plane_base = take(here)
    core_base = take(here + 1)
    piece = gb_ref.at[c, y, x]
    for j in range(here):
        start(piece, piece, plane_peer[j], plane_base + j)
    start(piece, piece, core_peer, core_base + here)
    sources = [
        (lax.rem(y + NY - o[1], NY), lax.rem(x + NX - o[0], NX)) for o in plane + [(0, 0)]
    ]
    for j in reversed(range(here)):
        piece = gb_ref.at[c, sources[j][0], sources[j][1]]
        copy(piece, piece, plane_peer[j], plane_base + j).wait_recv()
        start(piece, piece, core_peer, core_base + j)
    for j in reversed(range(here + 1)):
        piece = gb_ref.at[1 - c, sources[j][0], sources[j][1]]
        copy(piece, piece, core_peer, core_base + j).wait_recv()
    for j, o in enumerate(column):
        source = grad_ref.at[lax.rem(y + NY - o, NY)]
        copy(source, source, device(0, o, 0, 0), column_base + j).wait_recv()

    for descriptor in pending:
        descriptor.wait_send()


def write_kernel(
    sizes,
    gb_ref,
    grad_ref,
    master_ref,
    first_ref,
    second_ref,
    new_master_ref,
    new_first_ref,
    new_second_ref,
    out_ref,
    adam_ref,
):
    NX, NY, NZ, NB, W = sizes
    rows = NX * NZ * CORES
    half = NX * NZ
    r_at = lax.broadcasted_iota(jnp.int32, (rows, rows), 0)
    p_at = lax.broadcasted_iota(jnp.int32, (rows, rows), 1)
    back = (p_at == (r_at % CORES) * half + r_at // CORES).astype(F32).astype(BF16)
    done = 0
    for at in range(NY):
        begin = piece_start(sizes, at)
        for k in range(W):
            lo = (begin + k) * HAD
            adam_ref[0, k : k + 1, :] = master_ref[0:1, lo : lo + HAD]
            adam_ref[1, k : k + 1, :] = first_ref[0:1, lo : lo + HAD]
            adam_ref[2, k : k + 1, :] = second_ref[0:1, lo : lo + HAD]
        results = adam(grad_ref[at], adam_ref[0], adam_ref[1], adam_ref[2])
        for k in range(done - begin, W):
            lo = (begin + k) * HAD
            for ref, value in zip((new_master_ref, new_first_ref, new_second_ref), results):
                ref[0:1, lo : lo + HAD] = value[k : k + 1, :]
            cols = slice(k * HAD, (k + 1) * HAD)
            block = gb_ref[:, at, :, :, cols].reshape(rows, HAD)
            out_ref[:, lo : lo + HAD] = dot(back, block).astype(BF16)
        done = begin + W


def build(mesh, NX, NZ, NB):
    NY = mesh.shape["outer"]
    W = -(-NB // NY)
    sizes = (NX, NY, NZ, NB, W)
    rows = NX * NZ * CORES
    pair = CORES * NZ
    n_plane = NX * NY - 1
    n_line = NZ - 1
    messages = n_plane + n_plane + 1 + n_line + W + n_line
    messages += n_line + (NY - 1) + n_plane + n_plane + 1
    width = NB * HAD
    piece = W * HAD
    scratch = [
        pltpu.VMEM((rows, width), BF16),
        pltpu.VMEM((HAD, HAD), BF16),
        pltpu.VMEM((HAD, HAD), BF16),
        pltpu.VMEM((3, NY, W, HAD), F32),
        pltpu.VMEM((NY, NX, pair, piece), BF16),
        pltpu.VMEM((n_plane + 1, pair, piece), BF16),
        pltpu.VMEM((n_plane + 1, pair, piece), F32),
        pltpu.VMEM((NY, NX, CORES, LANES), F32),
        pltpu.VMEM((n_plane, CORES, LANES), F32),
        pltpu.VMEM((CORES, LANES), F32),
        pltpu.VMEM((CORES, LANES), F32),
        pltpu.VMEM((CORES, LANES), F32),
        pltpu.VMEM((n_line, CORES, LANES), F32),
        pltpu.VMEM((CORES, NZ, piece), F32),
        pltpu.VMEM((NZ, piece), F32),
        pltpu.VMEM((NZ, 2 * W, LANES), F32),
        pltpu.VMEM((n_line, 2 * W, LANES), F32),
        pltpu.VMEM((NZ, 2 * W, LANES), F32),
        pltpu.SemaphoreType.DMA,
        pltpu.SemaphoreType.DMA((messages,)),
        pltpu.SemaphoreType.DMA((messages,)),
    ]
    vmem = pl.BlockSpec(memory_space=pltpu.VMEM)
    row = jax.ShapeDtypeStruct((1, width), F32)

    def per_device(replica_grads, hadamard_signs, master_rows, first_moment, second_moment):
        gathered, gradients = pl.pallas_call(
            functools.partial(exchange_kernel, sizes),
            out_shape=(
                jax.ShapeDtypeStruct((CORES, NY, NX, NZ, piece), BF16),
                jax.ShapeDtypeStruct((NY, W, HAD), F32),
            ),
            in_specs=[pl.BlockSpec(memory_space=pltpu.HBM)] + [vmem] * 4,
            out_specs=(vmem, vmem),
            scratch_shapes=scratch,
            compiler_params=pltpu.CompilerParams(
                collective_id=0, has_side_effects=True, vmem_limit_bytes=40 * 2**20
            ),
        )(
            replica_grads,
            hadamard_signs.reshape(1, HAD),
            master_rows,
            first_moment,
            second_moment,
        )
        return pl.pallas_call(
            functools.partial(write_kernel, sizes),
            out_shape=(row, row, row, jax.ShapeDtypeStruct((rows, width), BF16)),
            in_specs=[vmem] * 5,
            out_specs=(vmem,) * 4,
            scratch_shapes=[pltpu.VMEM((3, W, HAD), F32)],
            compiler_params=pltpu.CompilerParams(vmem_limit_bytes=20 * 2**20),
        )(gathered, gradients, master_rows, first_moment, second_moment)

    in_specs = (P("dp", "outer", None, None), P(), P("dp", None), P("dp", None), P("dp", None))
    out_specs = (P("dp", None), P("dp", None), P("dp", None), P())
    return jax.shard_map(
        per_device, mesh=mesh, in_specs=in_specs, out_specs=out_specs, check_vma=False
    )


def solution(mesh):
    return build(mesh, 4, 16, 18)
```

time: 638 us -> 73.5 us (0.12)
  waiting for transfers between devices: 482 us -> 0 us
  blocking collectives: 124 us -> 0 us
  Pallas kernels: 0 us -> 68.4 us
  between operations: 14.3 us -> 0.65 us
  local copies, waits for them, and re-layouts: 10.8 us -> 4.11 us
    unnamed x3 -> x0, waiting for transfers between devices: 342 us -> none
    all_gather x1 -> x0, waiting for transfers between devices: 141 us -> none  [per_device(): lax.all_gather(new_master.astype(jnp.bfloat16), 'dp', axis=0, tiled=True)]
    pmax x1 -> x0, blocking collectives: 111 us -> none  [per_device(): block_peak = lax.pmax(meansq, ('dp', 'outer'))]
    pallas_call x0 -> x2, Pallas kernels: none -> 68.4 us  [the longest x1 66.9 us: per_device(): pl.pallas_call(functools.partial(exchange_kernel, sizes), out_shape=(jax....]
    psum x1 -> x0, blocking collectives: 13.2 us -> none  [per_device(): combined = lax.psum(terms, 'outer')]
  transfers between devices with their start and end apart: 2 -> 0, of which waited for: 2 -> 0; matrix products, arithmetic and copies ran while one was open for 0% -> 0% of each run, Pallas kernels for 0% -> 0%
where the time goes in v2:
time: 73.5 us; the launch traced here: 73.2 us
  Pallas kernels  68.4 us (93%)
  local copies, waits for them, and re-layouts  4.11 us (6%)
    pallas_call x1, Pallas kernels, per_device(): pl.pallas_call(functools.partial(exchange_kernel, sizes), out_shape=(jax....  66.9 us
    unnamed x10, local copies, waits for them, and re-layouts  4.11 us
    pallas_call x1, Pallas kernels, per_device(): pl.pallas_call(functools.partial(write_kernel, sizes), out_shape=(row, ro...  1.48 us

profile of v2, /device:TPU:1, one launch (start us, length us, event | category | flops | bytes accessed | tf_op | source)
XLA Modules:
  0.0 73.2 jit_solution(13558293592319028406)
XLA Ops:
  0.6 0.0 copy-start
  0.6 1.3 %copy-done = bf16[1,1,128,4608]{3,2,1,0:T(8,128)(2,1)S(1)} copy-done((bf16[1,1,128,4608]{3,2,1,0:T(8,128)(2,1)S(1)}, bf16[1,1,128,4608]{3,2,1,0:T(8,128)(2,1)}, u32[]{:S(2)}) %copy-start) | copy-done | bytes 1179672
  1.9 0.0 copy-start.1
  1.9 0.7 copy-done.1
  2.6 0.0 copy-start.2
  2.6 0.7 copy-done.2
  3.3 0.0 copy-start.3
  3.4 0.7 copy-done.3
  4.1 0.0 copy-start.4
  4.1 0.7 copy-done.4
  4.8 66.9 %shard_map.84 = (bf16[2,4,4,16,1280]{4,3,2,1,0:T(8,128)(2,1)S(1)}, f32[4,5,256]{2,1,0:T(8,128)S(1)}) custom-call(bf16[1,1,128,4608]{3,2,1,0:T(8,128)(2,1)S(1)} %copy-done, s32[1,256]{1,0:T(1,128)S(1)} %bitcast.1, f32[1,4608]{1,0:T(1,128)S(1)} %copy-done.1, f32[1,4608]{1,0:T(1,128)S(1)} %copy-done.2, f32[1,4608]{1,0:T(1,128)S(1)} %copy-done.3), custom_call_target="tpu_custom_call" | custom-call | tf_op jit(solution)/shard_map/pallas_call | solution.py:440
  71.7 1.5 %shard_map.85 = (f32[1,4608]{1,0:T(1,128)}, f32[1,4608]{1,0:T(1,128)}, f32[1,4608]{1,0:T(1,128)}, bf16[128,4608]{1,0:T(8,128)(2,1)}) custom-call(bf16[2,4,4,16,1280]{4,3,2,1,0:T(8,128)(2,1)S(1)} %get-tuple-element.6.gb_ref, f32[4,5,256]{2,1,0:T(8,128)S(1)} %get-tuple-element.7.grad_ref, f32[1,4608]{1,0:T(1,128)S(1)} %copy-done.1, f32[1,4608]{1,0:T(1,128)S(1)} %copy-done.2, ...), custom_call_target="tpu_custom_call" | custom-call | tf_op jit(solution)/shard_map/pallas_call | solution.py:459
Async XLA Ops:
  0.6 1.3 %copy-start = (bf16[1,1,128,4608]{3,2,1,0:T(8,128)(2,1)S(1)}, bf16[1,1,128,4608]{3,2,1,0:T(8,128)(2,1)}, u32[]{:S(2)}) copy-start(bf16[1,1,128,4608]{3,2,1,0:T(8,128)(2,1)} %grads_hbm.1) | copy-start | bytes 3538948
  1.9 0.7 copy-start.1
  2.6 0.7 copy-start.2
  3.3 0.7 copy-start.3
  4.1 0.7 copy-start.4

commit v3 on v2

v3 whole, which is shorter than its diff:
```python
import functools

import jax
import jax.numpy as jnp
from jax import lax
from jax.experimental import pallas as pl
from jax.experimental.pallas import tpu as pltpu
from jax.sharding import PartitionSpec as P

HAD = 256
LANES = 128
STEP = 1000
CORES = 2

beta_one = 0.9
beta_two = 0.95
rate = 0.001
decay = 0.1
tiny_eps = 1e-08
clip_level = 1.5
first_fix = 1.0 - beta_one**STEP
second_fix = 1.0 - beta_two**STEP

F32 = jnp.float32
BF16 = jnp.bfloat16
MESH = pl.DeviceIdType.MESH


def ring_distance(offset, size):
    return min(offset, size - offset)


def hadamard(dtype):
    bits = lax.broadcasted_iota(jnp.int32, (HAD, HAD), 0) & lax.broadcasted_iota(
        jnp.int32, (HAD, HAD), 1
    )
    bits = bits ^ (bits >> 4)
    bits = bits ^ (bits >> 2)
    bits = bits ^ (bits >> 1)
    return (1 - 2 * (bits & 1)).astype(F32).astype(dtype)


def split_three(value):
    high = value.astype(BF16)
    rest = value - high.astype(F32)
    middle = rest.astype(BF16)
    low = (rest - middle.astype(F32)).astype(BF16)
    return high, middle, low


def dot(a, b):
    return jnp.dot(a, b, preferred_element_type=F32)


def adam(gradient, master, first, second):
    new_first = beta_one * first + (1.0 - beta_one) * gradient
    new_second = beta_two * second + (1.0 - beta_two) * gradient * gradient
    update = (
        new_first * (1.0 / first_fix) / (jnp.sqrt(new_second * (1.0 / second_fix)) + tiny_eps)
        + decay * master
    )
    return master - rate * update, new_first, new_second


def piece_start(sizes, at):
    NX, NY, NZ, NB, W = sizes
    return (at * (NB - W) + NY - 2) // (NY - 1)


def plane_offsets(NX, NY):
    plane = [(ox, oy) for oy in range(NY) for ox in range(NX) if ox or oy]
    return sorted(plane, key=lambda o: -plane_hops(NX, NY, o))


def plane_hops(NX, NY, o):
    return ring_distance(o[0], NX) + ring_distance(o[1], NY)


def line_offsets(NZ):
    back = max(NZ // 4 - 1, 0)
    near = [o for o in range(-back, NZ // 2 - back) if o]
    far = list(range(NZ // 2 - back, NZ - back))
    return near, far


def exchange_kernel(
    sizes,
    grads_hbm,
    signs_hbm,
    master_hbm,
    first_hbm,
    second_hbm,
    gb_ref,
    grad_ref,
    x_ref,
    signs_ref,
    state_ref,
    table_ref,
    signed_ref,
    adam_ref,
    bulka_ref,
    bulkb_ref,
    rbulka_ref,
    rbulkb_ref,
    rota_ref,
    rotb_ref,
    m1_ref,
    r1_ref,
    m2_ref,
    r2_ref,
    m3_ref,
    r3_ref,
    acc_ref,
    racc_ref,
    zs_ref,
    rz_ref,
    near_ref,
    far_ref,
    load_sems,
    send_sems,
    recv_sems,
):
    NX, NY, NZ, NB, W = sizes
    rows = NX * NZ * CORES
    pair = CORES * NZ
    stride = LANES // NZ

    dp = lax.axis_index("dp")
    y = lax.axis_index("outer")
    c = lax.rem(dp, CORES)
    z = lax.rem(dp // CORES, NZ)
    x = dp // (CORES * NZ)

    def first_block(at):
        return piece_start(sizes, at)

    def device(dx, dy, dz, dc):
        px = lax.rem(x + dx, NX)
        py = lax.rem(y + dy, NY)
        pz = lax.rem(z + dz, NZ)
        pc = lax.rem(c + dc, CORES)
        return ((px * NZ + pz) * CORES + pc, py)

    plane = plane_offsets(NX, NY)
    near, far = line_offsets(NZ)
    line = sorted([o % NZ for o in near + far], key=lambda o: -ring_distance(o, NZ))
    column = list(range(1, NY))
    core_peer = device(0, 0, 0, 1)
    plane_peer = [device(o[0], o[1], 0, 0) for o in plane]
    line_peer = {o: device(0, 0, o, 0) for o in line}
    here = len(plane)
    WA = (W + 1) // 2

    barrier = pltpu.get_barrier_semaphore()
    peers = [line_peer[o] for o in line] + plane_peer + [core_peer]
    for peer in peers:
        pl.semaphore_signal(barrier, inc=1, device_id=peer, device_id_type=MESH)

    begin = pl.multiple_of(first_block(y) * HAD, HAD)
    loads = [
        pltpu.make_async_copy(grads_hbm.at[0, 0], x_ref, load_sems.at[0]),
        pltpu.make_async_copy(signs_hbm, signs_ref, load_sems.at[1]),
    ]
    for i, hbm in enumerate((master_hbm, first_hbm, second_hbm)):
        loads.append(
            pltpu.make_async_copy(
                hbm.at[:, pl.ds(begin, W * HAD)], state_ref.at[i], load_sems.at[2 + i]
            )
        )
    for load in loads:
        load.start()

    counter = [0]
    sent = []

    def copy(src, dst, peer, send, recv):
        return pltpu.make_async_remote_copy(
            src_ref=src,
            dst_ref=dst,
            send_sem=send_sems.at[send],
            recv_sem=recv_sems.at[recv],
            device_id=peer,
            device_id_type=MESH,
        )

    def stage():
        counter[0] += 1
        return counter[0] - 1

    def landed(ref, index):
        copy(ref, ref, core_peer, index, index).wait_recv()

    p_at = lax.broadcasted_iota(jnp.int32, (rows, rows), 0)
    r_at = lax.broadcasted_iota(jnp.int32, (rows, rows), 1)
    r_core = r_at % CORES
    r_z = (r_at // CORES) % NZ
    r_x = r_at // pair
    order = (p_at == r_x * pair + r_core * NZ + r_z).astype(F32).astype(BF16)

    table = hadamard(BF16)
    table_ref[...] = table

    loads[0].wait()

    lane = lax.broadcasted_iota(jnp.int32, (HAD, LANES), 1)
    picks = [(lane % stride == k).astype(F32).astype(BF16) for k in range(W)]
    sums = [jnp.zeros((rows, LANES), F32) for _ in range(NY)]
    for block in range(NB):
        value = dot(order, x_ref[:, block * HAD : (block + 1) * HAD])
        square = value * value
        high = square.astype(BF16)
        low = (square - high.astype(F32)).astype(BF16)
        both = jnp.concatenate([high, low], axis=0)
        value = value.astype(BF16).reshape(NX, pair, HAD)
        for at in range(NY):
            k = block - first_block(at)
            if 0 <= k < W:
                part = dot(both, picks[k])
                sums[at] = sums[at] + (part[0:rows] + part[rows : 2 * rows])
                if k < WA:
                    bulka_ref[at, :, :, k * HAD : (k + 1) * HAD] = value
                else:
                    bulkb_ref[at, :, :, (k - WA) * HAD : (k - WA + 1) * HAD] = value
    row_at = lax.broadcasted_iota(jnp.int32, (rows, LANES), 0)
    lane_at = lax.broadcasted_iota(jnp.int32, (rows, LANES), 1)
    mine = row_at % NZ == lane_at // stride
    for at in range(NY):
        packed = jnp.where(mine, sums[at], 0.0).reshape(NX * CORES, NZ, LANES)
        packed = jnp.sum(packed, axis=1) * (1.0 / HAD)
        for px in range(NX):
            m1_ref[at, px] = packed[px * CORES : (px + 1) * CORES]

    pl.semaphore_wait(barrier, len(peers))

    def over_plane(parts_ref, slots_ref):
        index = stage()
        for j, o in enumerate(plane):
            piece = parts_ref.at[lax.rem(y + o[1], NY), lax.rem(x + o[0], NX)]
            copy(piece, slots_ref.at[j], plane_peer[j], index, index).start()
        sent.append((slots_ref.at[0:here], index))
        return index

    first_maxima = over_plane(m1_ref, r1_ref)
    wave_a = over_plane(bulka_ref, rbulka_ref)
    rbulka_ref[here] = bulka_ref[y, x]
    rbulkb_ref[here] = bulkb_ref[y, x]

    diagonal = lax.broadcasted_iota(jnp.int32, (HAD, HAD), 0) == lax.broadcasted_iota(
        jnp.int32, (HAD, HAD), 1
    )
    for load in loads[1:]:
        load.wait()
    sign_row = signs_ref[...].astype(F32)
    signed_ref[...] = dot(
        jnp.where(diagonal, sign_row, 0.0).astype(BF16), table
    ).astype(BF16)
    for k in range(W):
        for i in range(3):
            adam_ref[i, k : k + 1, :] = state_ref[i, :, k * HAD : (k + 1) * HAD]

    landed(r1_ref, first_maxima)
    peak = jnp.maximum(m1_ref[y, x], jnp.max(r1_ref[...], axis=0))
    m2_ref[...] = peak
    index = stage()
    copy(m2_ref, r2_ref, core_peer, index, index).start()
    sent.append((r2_ref, index))
    landed(r2_ref, index)
    peak = jnp.maximum(peak, r2_ref[...])
    m3_ref[...] = peak
    last_maxima = stage()
    for j, o in enumerate(line):
        copy(m3_ref, r3_ref.at[j], line_peer[o], last_maxima, last_maxima).start()
    sent.append((r3_ref, last_maxima))

    signed = signed_ref[...]

    def rotate(slots_ref, out_ref, count):
        for k in range(count):
            cols = slice(k * HAD, (k + 1) * HAD)
            value = slots_ref[:, :, cols].reshape((here + 1) * pair, HAD)
            out_ref[:, :, cols] = dot(value, signed).reshape(here + 1, pair, HAD)

    landed(rbulka_ref.at[0:here], wave_a)
    wave_b = over_plane(bulkb_ref, rbulkb_ref)
    rotate(rbulka_ref, rota_ref, WA)
    landed(rbulkb_ref.at[0:here], wave_b)
    rotate(rbulkb_ref, rotb_ref, W - WA)

    landed(r3_ref, last_maxima)
    peak = jnp.maximum(peak, jnp.max(r3_ref[...], axis=0))

    scales = jnp.sqrt(peak + 1e-06)
    inverse = 0.0625 / scales
    z_at = lax.broadcasted_iota(jnp.int32, (NZ, LANES), 0)
    l_at = lax.broadcasted_iota(jnp.int32, (NZ, LANES), 1)
    core_send = stage()
    core_recv = [stage() for _ in range(W)]
    for k in range(W):
        cols = slice(k * HAD, (k + 1) * HAD)
        pick = l_at == z_at * stride + k
        factor = jnp.concatenate(
            [
                jnp.sum(
                    jnp.where(pick, jnp.broadcast_to(inverse[g : g + 1], (NZ, LANES)), 0.0),
                    axis=1,
                    keepdims=True,
                )
                for g in range(CORES)
            ],
            axis=0,
        )
        factor = jnp.broadcast_to(factor, (pair, HAD))
        total = jnp.zeros((pair, HAD), F32)
        rot_ref, at = (rota_ref, k) if k < WA else (rotb_ref, k - WA)
        for j in range(here + 1):
            value = rot_ref[j, :, at * HAD : (at + 1) * HAD] * factor
            value = jnp.clip(value, -clip_level, clip_level)
            total = total + value.astype(BF16).astype(F32)
        acc_ref[0, :, cols] = total[0:NZ]
        acc_ref[1, :, cols] = total[NZ:pair]
        copy(
            acc_ref.at[1 - c, :, cols], racc_ref.at[:, cols], core_peer, core_send, core_recv[k]
        ).start()
    sent.append((racc_ref, core_send))

    w_at = lax.broadcasted_iota(jnp.int32, (W, LANES), 0)
    k_at = lax.broadcasted_iota(jnp.int32, (W, LANES), 1)
    own = jnp.broadcast_to(jnp.where(c == 0, scales[0:1], scales[1:2]), (W, LANES))
    own_scale = jnp.sum(
        jnp.where(k_at == z * stride + w_at, own, 0.0), axis=1, keepdims=True
    )

    for k in range(W):
        landed(racc_ref.at[:, k * HAD : (k + 1) * HAD], core_recv[k])
        for h in range(2):
            cols = slice(k * HAD + h * LANES, k * HAD + (h + 1) * LANES)
            zs_ref[:, h * W + k, :] = acc_ref[c, :, cols] + racc_ref[:, cols]

    index = stage()
    for j, o in enumerate(line):
        copy(
            zs_ref.at[lax.rem(z + o, NZ)], rz_ref.at[j], line_peer[o], index, index
        ).start()
    sent.append((rz_ref, index))
    own_part = zs_ref[z]
    landed(rz_ref, index)
    total = own_part + jnp.sum(rz_ref[...], axis=0)

    wide = jnp.concatenate([total[0:W], total[W : 2 * W]], axis=1)
    parts = split_three(wide * own_scale)
    table = table_ref[...]
    gradient = (dot(parts[0], table) + dot(parts[1], table)) + dot(parts[2], table)
    gradient = gradient * 0.0625 * sign_row
    grad_ref[y] = gradient
    updated, _, _ = adam(gradient, adam_ref[0], adam_ref[1], adam_ref[2])
    updated = updated.astype(BF16).astype(F32)
    near_ref[len(near), 0:W] = updated[:, 0:LANES]
    near_ref[len(near), W : 2 * W] = updated[:, LANES:HAD]

    far_sem = stage()
    near_sem = stage()
    mine = near_ref.at[len(near)]
    slots = {o % NZ: (near_ref.at[i], near_sem) for i, o in enumerate(near)}
    slots.update({o % NZ: (far_ref.at[i], far_sem) for i, o in enumerate(far)})
    for o in line:
        slot, index = slots[o]
        copy(mine, slot, line_peer[o], index, index).start()
    sent.append((far_ref, far_sem))
    if near:
        sent.append((near_ref.at[0 : len(near)], near_sem))
    column_sem = stage()
    for o in column:
        copy(
            grad_ref.at[y], grad_ref.at[y], device(0, o, 0, 0), column_sem, column_sem
        ).start()
    sent.append((grad_ref.at[0 : NY - 1], column_sem))

    groups = []
    for j, o in enumerate(plane):
        if j and plane_hops(NX, NY, plane[j - 1]) == plane_hops(NX, NY, o):
            groups[-1][1] = j + 1
        else:
            groups.append([j, j + 1])
    core_sem = stage()

    def share(part, rows_ref):
        for k in range(W):
            both = jnp.concatenate([rows_ref[:, k, :], rows_ref[:, W + k, :]], axis=0)
            gb_ref[c, part, here, :, k * LANES : (k + 1) * LANES] = both.astype(BF16)
        send = stage()
        recv = {}
        for lo, hi in groups:
            index = stage()
            recv[lo] = index
            for j in range(lo, hi):
                copy(
                    gb_ref.at[c, part, here], gb_ref.at[c, part, j], plane_peer[j], send, index
                ).start()
        sent.append((gb_ref.at[c, part, 0:here], send))
        return recv

    def pass_on(part, recv):
        for lo, hi in reversed(groups):
            landed(gb_ref.at[c, part, lo:hi], recv[lo])
            hi = here + 1 if hi == here else hi
            piece = gb_ref.at[c, part, lo:hi]
            copy(piece, piece, core_peer, core_sem, core_sem).start()

    if near:
        landed(near_ref.at[0 : len(near)], near_sem)
    recv_near = share(0, near_ref)
    landed(far_ref, far_sem)
    recv_far = share(1, far_ref)
    pass_on(0, recv_near)
    pass_on(1, recv_far)
    landed(grad_ref.at[0 : NY - 1], column_sem)
    landed(gb_ref.at[1 - c], core_sem)
    sent.append((gb_ref.at[c], core_sem))

    for ref, index in sent:
        copy(ref, ref, core_peer, index, index).wait_send()


def write_kernel(
    sizes,
    gb_ref,
    grad_ref,
    master_ref,
    first_ref,
    second_ref,
    new_master_ref,
    new_first_ref,
    new_second_ref,
    out_ref,
    adam_ref,
):
    NX, NY, NZ, NB, W = sizes
    rows = NX * NZ * CORES
    plane = plane_offsets(NX, NY)
    slot_of = {o: j for j, o in enumerate(plane + [(0, 0)])}
    near, far = line_offsets(NZ)
    dp = lax.axis_index("dp")
    y = lax.axis_index("outer")
    z = lax.rem(dp // CORES, NZ)
    x = dp // (CORES * NZ)

    for at in range(NY):
        begin = piece_start(sizes, at)
        for k in range(W):
            lo = (begin + k) * HAD
            adam_ref[0, k : k + 1, :] = master_ref[0:1, lo : lo + HAD]
            adam_ref[1, k : k + 1, :] = first_ref[0:1, lo : lo + HAD]
            adam_ref[2, k : k + 1, :] = second_ref[0:1, lo : lo + HAD]
        results = adam(grad_ref[at], adam_ref[0], adam_ref[1], adam_ref[2])
        end = piece_start(sizes, at + 1) if at < NY - 1 else NB
        for k in range(end - begin):
            lo = (begin + k) * HAD
            for ref, value in zip((new_master_ref, new_first_ref, new_second_ref), results):
                ref[0:1, lo : lo + HAD] = value[k : k + 1, :]

    shape = (rows, CORES * 2 * NX * NZ)
    r_at = lax.broadcasted_iota(jnp.int32, shape, 0)
    g_at = lax.broadcasted_iota(jnp.int32, shape, 1)
    low = g_at % (NZ // 2)
    second_half = (g_at // (NZ // 2)) % 2
    ox = (g_at // NZ) % NX
    part = (g_at // (NZ * NX)) % 2
    core = g_at // (NZ * NX * 2)
    back = max(NZ // 4 - 1, 0)
    near_o = jnp.where(low == len(near), 0, low - back + (low >= back).astype(jnp.int32))
    oz = jnp.where(part == 0, near_o, low + NZ // 2 - back)
    source = (((x - ox + NX) % NX) * NZ + (z - oz + NZ) % NZ) * CORES + core
    pick = [
        ((r_at == source) & (second_half == h)).astype(F32).astype(BF16) for h in range(2)
    ]
    for oy in range(NY):
        at = lax.rem(y + NY - oy, NY)
        begin = piece_start(sizes, at) * HAD
        value = jnp.concatenate(
            [
                gb_ref[core, part, slot_of[(ox, oy)]]
                for core in range(CORES)
                for part in range(2)
                for ox in range(NX)
            ],
            axis=0,
        )
        tiles = [dot(pick[h], value).astype(BF16) for h in range(2)]
        for k in range(W):
            both = jnp.concatenate(
                [tile[:, k * LANES : (k + 1) * LANES] for tile in tiles], axis=1
            )
            cols = pl.ds(pl.multiple_of(begin + k * HAD, HAD), HAD)
            if k < W - 1:
                out_ref[:, cols] = both
            else:

                @pl.when((at == 0) | (at == NY - 1))
                def _():
                    out_ref[:, cols] = both


def build(mesh, NX, NZ, NB):
    NY = mesh.shape["outer"]
    W = -(-NB // NY)
    sizes = (NX, NY, NZ, NB, W)
    rows = NX * NZ * CORES
    pair = CORES * NZ
    n_plane = NX * NY - 1
    n_line = NZ - 1
    groups = len({plane_hops(NX, NY, o) for o in plane_offsets(NX, NY)})
    stages = 12 + W + 2 * (groups + 1)
    near, far = line_offsets(NZ)
    WA = (W + 1) // 2
    width = NB * HAD
    piece = W * HAD
    scratch = [
        pltpu.VMEM((rows, width), BF16),
        pltpu.VMEM((1, HAD), jnp.int32),
        pltpu.VMEM((3, 1, piece), F32),
        pltpu.VMEM((HAD, HAD), BF16),
        pltpu.VMEM((HAD, HAD), BF16),
        pltpu.VMEM((3, W, HAD), F32),
        pltpu.VMEM((NY, NX, pair, WA * HAD), BF16),
        pltpu.VMEM((NY, NX, pair, (W - WA) * HAD), BF16),
        pltpu.VMEM((n_plane + 1, pair, WA * HAD), BF16),
        pltpu.VMEM((n_plane + 1, pair, (W - WA) * HAD), BF16),
        pltpu.VMEM((n_plane + 1, pair, WA * HAD), F32),
        pltpu.VMEM((n_plane + 1, pair, (W - WA) * HAD), F32),
        pltpu.VMEM((NY, NX, CORES, LANES), F32),
        pltpu.VMEM((n_plane, CORES, LANES), F32),
        pltpu.VMEM((CORES, LANES), F32),
        pltpu.VMEM((CORES, LANES), F32),
        pltpu.VMEM((CORES, LANES), F32),
        pltpu.VMEM((n_line, CORES, LANES), F32),
        pltpu.VMEM((CORES, NZ, piece), F32),
        pltpu.VMEM((NZ, piece), F32),
        pltpu.VMEM((NZ, 2 * W, LANES), F32),
        pltpu.VMEM((n_line, 2 * W, LANES), F32),
        pltpu.VMEM((len(near) + 1, 2 * W, LANES), F32),
        pltpu.VMEM((len(far), 2 * W, LANES), F32),
        pltpu.SemaphoreType.DMA((5,)),
        pltpu.SemaphoreType.DMA((stages,)),
        pltpu.SemaphoreType.DMA((stages,)),
    ]
    vmem = pl.BlockSpec(memory_space=pltpu.VMEM)
    row = jax.ShapeDtypeStruct((1, width), F32)

    def per_device(replica_grads, hadamard_signs, master_rows, first_moment, second_moment):
        gathered, gradients = pl.pallas_call(
            functools.partial(exchange_kernel, sizes),
            out_shape=(
                pltpu.VMEM((CORES, 2, n_plane + 1, NZ, piece // 2), BF16),
                pltpu.VMEM((NY, W, HAD), F32),
            ),
            in_specs=[pl.BlockSpec(memory_space=pltpu.HBM)] * 5,
            out_specs=(vmem, vmem),
            scratch_shapes=scratch,
            compiler_params=pltpu.CompilerParams(
                collective_id=0, has_side_effects=True, vmem_limit_bytes=40 * 2**20
            ),
        )(
            *[
                pltpu.with_memory_space_constraint(array, pltpu.HBM)
                for array in (
                    replica_grads,
                    hadamard_signs.reshape(1, HAD),
                    master_rows,
                    first_moment,
                    second_moment,
                )
            ]
        )
        return pl.pallas_call(
            functools.partial(write_kernel, sizes),
            out_shape=(row, row, row, jax.ShapeDtypeStruct((rows, width), BF16)),
            in_specs=[vmem] * 5,
            out_specs=(vmem,) * 4,
            scratch_shapes=[pltpu.VMEM((3, W, HAD), F32)],
            compiler_params=pltpu.CompilerParams(vmem_limit_bytes=20 * 2**20),
        )(gathered, gradients, master_rows, first_moment, second_moment)

    in_specs = (P("dp", "outer", None, None), P(), P("dp", None), P("dp", None), P("dp", None))
    out_specs = (P("dp", None), P("dp", None), P("dp", None), P())
    return jax.shard_map(
        per_device, mesh=mesh, in_specs=in_specs, out_specs=out_specs, check_vma=False
    )


def solution(mesh):
    return build(mesh, 4, 16, 18)
```

time: 73.5 us -> 65.3 us (0.89)
  local copies, waits for them, and re-layouts: 4.11 us -> 0.01 us
  Pallas kernels: 68.4 us -> 64.4 us
    pallas_call x1, Pallas kernels: 66.9 us -> 62.2 us  [per_device(): pl.pallas_call(functools.partial(exchange_kernel, sizes), out_shape=(pltp...]
    unnamed x10 -> x6, local copies, waits for them, and re-layouts: 4.11 us -> 0.01 us
    pallas_call x1, Pallas kernels: 1.48 us -> 2.22 us  [per_device(): pl.pallas_call(functools.partial(write_kernel, sizes), out_shape=(row, ro...]
where the time goes in v3:
time: 65.3 us; the launch traced here: 65.1 us
  Pallas kernels  64.4 us (99%)
  between operations  0.69 us (1%)
    pallas_call x1, Pallas kernels, per_device(): pl.pallas_call(functools.partial(exchange_kernel, sizes), out_shape=(pltp...  62.2 us
    pallas_call x1, Pallas kernels, per_device(): pl.pallas_call(functools.partial(write_kernel, sizes), out_shape=(row, ro...  2.22 us

profile of v3, /device:TPU:1, one launch (start us, length us, event | category | flops | bytes accessed | tf_op | source)
XLA Modules:
  0.0 65.1 jit_solution(5126837365330765112)
XLA Ops:
  0.6 0.0 copy-start.2
  0.6 0.0 copy-start.1
  0.7 0.0 copy-start
  0.7 62.2 %shard_map.84 = (bf16[2,2,16,16,640]{4,3,2,1,0:T(8,128)(2,1)S(1)}, f32[4,5,256]{2,1,0:T(8,128)S(1)}) custom-call(bf16[1,1,128,4608]{3,2,1,0:T(8,128)(2,1)} %grads_hbm.1, s32[1,256]{1,0:T(1,128)} %bitcast.1, f32[1,4608]{1,0:T(1,128)} %master_ref.1, f32[1,4608]{1,0:T(1,128)} %first_ref.1, f32[1,4608]{1,0:T(1,128)} %second_ref.1), custom_call_target="tpu_custom_call" | custom-call | tf_op jit(solution)/shard_map/pallas_call | solution.py:550
  62.8 0.0 copy-done.2
  62.8 0.0 copy-done.1
  62.8 0.0 copy-done
  62.9 2.2 %shard_map.85 = (f32[1,4608]{1,0:T(1,128)}, f32[1,4608]{1,0:T(1,128)}, f32[1,4608]{1,0:T(1,128)}, bf16[128,4608]{1,0:T(8,128)(2,1)}) custom-call(bf16[2,2,16,16,640]{4,3,2,1,0:T(8,128)(2,1)S(1)} %get-tuple-element.6.gb_ref, f32[4,5,256]{2,1,0:T(8,128)S(1)} %get-tuple-element.7.grad_ref, f32[1,4608]{1,0:T(1,128)S(1)} %copy-done, f32[1,4608]{1,0:T(1,128)S(1)} %copy-done.1, ...), custom_call_target="tpu_custom_call" | custom-call | tf_op jit(solution)/shard_map/pallas_call | solution.py:574
Async XLA Ops:
  0.6 62.2 %copy-start.2 = (f32[1,4608]{1,0:T(1,128)S(1)}, f32[1,4608]{1,0:T(1,128)}, u32[]{:S(2)}) copy-start(f32[1,4608]{1,0:T(1,128)} %second_ref.1) | copy-start | bytes 55300
  0.6 62.2 %copy-start.1 = (f32[1,4608]{1,0:T(1,128)S(1)}, f32[1,4608]{1,0:T(1,128)}, u32[]{:S(2)}) copy-start(f32[1,4608]{1,0:T(1,128)} %first_ref.1) | copy-start | bytes 55300
  0.7 62.2 %copy-start = (f32[1,4608]{1,0:T(1,128)S(1)}, f32[1,4608]{1,0:T(1,128)}, u32[]{:S(2)}) copy-start(f32[1,4608]{1,0:T(1,128)} %master_ref.1) | copy-start | bytes 55300

commit v4 on v3

--- a/solution.py
+++ b/solution.py
@@ -98,12 +98,9 @@
     table_ref,
     signed_ref,
     adam_ref,
-    bulka_ref,
-    bulkb_ref,
-    rbulka_ref,
-    rbulkb_ref,
-    rota_ref,
-    rotb_ref,
+    bulk_ref,
+    rbulk_ref,
+    rot_ref,
     m1_ref,
     r1_ref,
     m2_ref,
@@ -149,7 +146,6 @@
     plane_peer = [device(o[0], o[1], 0, 0) for o in plane]
     line_peer = {o: device(0, 0, o, 0) for o in line}
     here = len(plane)
-    WA = (W + 1) // 2
 
     barrier = pltpu.get_barrier_semaphore()
     peers = [line_peer[o] for o in line] + plane_peer + [core_peer]
@@ -191,9 +187,9 @@
         copy(ref, ref, core_peer, index, index).wait_recv()
 
     p_at = lax.broadcasted_iota(jnp.int32, (rows, rows), 0)
-    r_at = lax.broadcasted_iota(jnp.int32, (rows, rows), 1)
-    r_core = r_at % CORES
-    r_z = (r_at // CORES) % NZ
+    r_at = lax.broadcasted_iota(jnp.int32, (1, rows), 1)
+    r_core = lax.rem(r_at, CORES)
+    r_z = lax.rem(r_at // CORES, NZ)
     r_x = r_at // pair
     order = (p_at == r_x * pair + r_core * NZ + r_z).astype(F32).astype(BF16)
 
@@ -202,8 +198,10 @@
 
     loads[0].wait()
 
-    lane = lax.broadcasted_iota(jnp.int32, (HAD, LANES), 1)
-    picks = [(lane % stride == k).astype(F32).astype(BF16) for k in range(W)]
+    lane = lax.rem(lax.broadcasted_iota(jnp.int32, (1, LANES), 1), stride)
+    picks = [
+        jnp.broadcast_to((lane == k).astype(F32), (HAD, LANES)).astype(BF16) for k in range(W)
+    ]
     sums = [jnp.zeros((rows, LANES), F32) for _ in range(NY)]
     for block in range(NB):
         value = dot(order, x_ref[:, block * HAD : (block + 1) * HAD])
@@ -217,10 +215,7 @@
             if 0 <= k < W:
                 part = dot(both, picks[k])
                 sums[at] = sums[at] + (part[0:rows] + part[rows : 2 * rows])
-                if k < WA:
-                    bulka_ref[at, :, :, k * HAD : (k + 1) * HAD] = value
-                else:
-                    bulkb_ref[at, :, :, (k - WA) * HAD : (k - WA + 1) * HAD] = value
+                bulk_ref[k, at] = value
     row_at = lax.broadcasted_iota(jnp.int32, (rows, LANES), 0)
     lane_at = lax.broadcasted_iota(jnp.int32, (rows, LANES), 1)
     mine = row_at % NZ == lane_at // stride
@@ -241,9 +236,10 @@
         return index
 
     first_maxima = over_plane(m1_ref, r1_ref)
-    wave_a = over_plane(bulka_ref, rbulka_ref)
-    rbulka_ref[here] = bulka_ref[y, x]
-    rbulkb_ref[here] = bulkb_ref[y, x]
+    ahead = 3
+    waves = [over_plane(bulk_ref.at[k], rbulk_ref.at[k]) for k in range(min(ahead, W))]
+    for k in range(W):
+        rbulk_ref[k, here] = bulk_ref[k, y, x]
 
     diagonal = lax.broadcasted_iota(jnp.int32, (HAD, HAD), 0) == lax.broadcasted_iota(
         jnp.int32, (HAD, HAD), 1
@@ -273,18 +269,12 @@
     sent.append((r3_ref, last_maxima))
 
     signed = signed_ref[...]
-
-    def rotate(slots_ref, out_ref, count):
-        for k in range(count):
-            cols = slice(k * HAD, (k + 1) * HAD)
-            value = slots_ref[:, :, cols].reshape((here + 1) * pair, HAD)
-            out_ref[:, :, cols] = dot(value, signed).reshape(here + 1, pair, HAD)
-
-    landed(rbulka_ref.at[0:here], wave_a)
-    wave_b = over_plane(bulkb_ref, rbulkb_ref)
-    rotate(rbulka_ref, rota_ref, WA)
-    landed(rbulkb_ref.at[0:here], wave_b)
-    rotate(rbulkb_ref, rotb_ref, W - WA)
+    for k in range(W):
+        landed(rbulk_ref.at[k, 0:here], waves[k])
+        if k + ahead < W:
+            waves.append(over_plane(bulk_ref.at[k + ahead], rbulk_ref.at[k + ahead]))
+        value = rbulk_ref[k].reshape((here + 1) * pair, HAD)
+        rot_ref[k] = dot(value, signed).reshape(here + 1, pair, HAD)
 
     landed(r3_ref, last_maxima)
     peak = jnp.maximum(peak, jnp.max(r3_ref[...], axis=0))
@@ -311,10 +301,8 @@
         )
         factor = jnp.broadcast_to(factor, (pair, HAD))
         total = jnp.zeros((pair, HAD), F32)
-        rot_ref, at = (rota_ref, k) if k < WA else (rotb_ref, k - WA)
         for j in range(here + 1):
-            value = rot_ref[j, :, at * HAD : (at + 1) * HAD] * factor
-            value = jnp.clip(value, -clip_level, clip_level)
+            value = jnp.clip(rot_ref[k, j] * factor, -clip_level, clip_level)
             total = total + value.astype(BF16).astype(F32)
         acc_ref[0, :, cols] = total[0:NZ]
         acc_ref[1, :, cols] = total[NZ:pair]
@@ -458,20 +446,21 @@
             for ref, value in zip((new_master_ref, new_first_ref, new_second_ref), results):
                 ref[0:1, lo : lo + HAD] = value[k : k + 1, :]
 
-    shape = (rows, CORES * 2 * NX * NZ)
-    r_at = lax.broadcasted_iota(jnp.int32, shape, 0)
-    g_at = lax.broadcasted_iota(jnp.int32, shape, 1)
-    low = g_at % (NZ // 2)
-    second_half = (g_at // (NZ // 2)) % 2
-    ox = (g_at // NZ) % NX
-    part = (g_at // (NZ * NX)) % 2
+    slots = CORES * 2 * NX * NZ
+    r_at = lax.broadcasted_iota(jnp.int32, (rows, slots), 0)
+    g_at = lax.broadcasted_iota(jnp.int32, (1, slots), 1)
+    low = lax.rem(g_at, NZ // 2)
+    second_half = lax.rem(g_at // (NZ // 2), 2)
+    ox = lax.rem(g_at // NZ, NX)
+    part = lax.rem(g_at // (NZ * NX), 2)
     core = g_at // (NZ * NX * 2)
     back = max(NZ // 4 - 1, 0)
     near_o = jnp.where(low == len(near), 0, low - back + (low >= back).astype(jnp.int32))
     oz = jnp.where(part == 0, near_o, low + NZ // 2 - back)
-    source = (((x - ox + NX) % NX) * NZ + (z - oz + NZ) % NZ) * CORES + core
+    source = (lax.rem(x - ox + NX, NX) * NZ + lax.rem(z - oz + NZ, NZ)) * CORES + core
     pick = [
-        ((r_at == source) & (second_half == h)).astype(F32).astype(BF16) for h in range(2)
+        (r_at == jnp.where(second_half == h, source, -1)).astype(F32).astype(BF16)
+        for h in range(2)
     ]
     for oy in range(NY):
         at = lax.rem(y + NY - oy, NY)
@@ -509,9 +498,8 @@
     n_plane = NX * NY - 1
     n_line = NZ - 1
     groups = len({plane_hops(NX, NY, o) for o in plane_offsets(NX, NY)})
-    stages = 12 + W + 2 * (groups + 1)
+    stages = 10 + 2 * W + 2 * (groups + 1)
     near, far = line_offsets(NZ)
-    WA = (W + 1) // 2
     width = NB * HAD
     piece = W * HAD
     scratch = [
@@ -521,12 +509,9 @@
         pltpu.VMEM((HAD, HAD), BF16),
         pltpu.VMEM((HAD, HAD), BF16),
         pltpu.VMEM((3, W, HAD), F32),
-        pltpu.VMEM((NY, NX, pair, WA * HAD), BF16),
-        pltpu.VMEM((NY, NX, pair, (W - WA) * HAD), BF16),
-        pltpu.VMEM((n_plane + 1, pair, WA * HAD), BF16),
-        pltpu.VMEM((n_plane + 1, pair, (W - WA) * HAD), BF16),
-        pltpu.VMEM((n_plane + 1, pair, WA * HAD), F32),
-        pltpu.VMEM((n_plane + 1, pair, (W - WA) * HAD), F32),
+        pltpu.VMEM((W, NY, NX, pair, HAD), BF16),
+        pltpu.VMEM((W, n_plane + 1, pair, HAD), BF16),
+        pltpu.VMEM((W, n_plane + 1, pair, HAD), F32),
         pltpu.VMEM((NY, NX, CORES, LANES), F32),
         pltpu.VMEM((n_plane, CORES, LANES), F32),
         pltpu.VMEM((CORES, LANES), F32),

time: 65.3 us -> 63.4 us (0.971)
  Pallas kernels: 64.4 us -> 62.6 us
    pallas_call x1, Pallas kernels: 62.2 us -> 60.3 us  [per_device(): pl.pallas_call(functools.partial(exchange_kernel, sizes), out_shape=(pltp...]
where the time goes in v4:
time: 63.4 us; the launch traced here: 63.3 us
  Pallas kernels  62.6 us (99%)
  between operations  0.69 us (1%)
    pallas_call x1, Pallas kernels, per_device(): pl.pallas_call(functools.partial(exchange_kernel, sizes), out_shape=(pltp...  60.3 us
    pallas_call x1, Pallas kernels, per_device(): pl.pallas_call(functools.partial(write_kernel, sizes), out_shape=(row, ro...  2.22 us

profile of v4, /device:TPU:1, one launch (start us, length us, event | category | flops | bytes accessed | tf_op | source)
XLA Modules:
  0.0 63.3 jit_solution(10228358720122125455)
XLA Ops:
  0.6 0.0 copy-start.2
  0.6 0.0 copy-start.1
  0.7 0.0 copy-start
  0.7 60.3 %shard_map.84 = (bf16[2,2,16,16,640]{4,3,2,1,0:T(8,128)(2,1)S(1)}, f32[4,5,256]{2,1,0:T(8,128)S(1)}) custom-call(bf16[1,1,128,4608]{3,2,1,0:T(8,128)(2,1)} %grads_hbm.1, s32[1,256]{1,0:T(1,128)} %bitcast.1, f32[1,4608]{1,0:T(1,128)} %master_ref.1, f32[1,4608]{1,0:T(1,128)} %first_ref.1, f32[1,4608]{1,0:T(1,128)} %second_ref.1), custom_call_target="tpu_custom_call" | custom-call | tf_op jit(solution)/shard_map/pallas_call | solution.py:535
  61.0 0.0 copy-done.2
  61.0 0.0 copy-done.1
  61.0 0.0 copy-done
  61.0 2.2 %shard_map.85 = (f32[1,4608]{1,0:T(1,128)}, f32[1,4608]{1,0:T(1,128)}, f32[1,4608]{1,0:T(1,128)}, bf16[128,4608]{1,0:T(8,128)(2,1)}) custom-call(bf16[2,2,16,16,640]{4,3,2,1,0:T(8,128)(2,1)S(1)} %get-tuple-element.6.gb_ref, f32[4,5,256]{2,1,0:T(8,128)S(1)} %get-tuple-element.7.grad_ref, f32[1,4608]{1,0:T(1,128)S(1)} %copy-done, f32[1,4608]{1,0:T(1,128)S(1)} %copy-done.1, ...), custom_call_target="tpu_custom_call" | custom-call | tf_op jit(solution)/shard_map/pallas_call | solution.py:559
Async XLA Ops:
  0.6 60.4 %copy-start.2 = (f32[1,4608]{1,0:T(1,128)S(1)}, f32[1,4608]{1,0:T(1,128)}, u32[]{:S(2)}) copy-start(f32[1,4608]{1,0:T(1,128)} %second_ref.1) | copy-start | bytes 55300
  0.6 60.4 %copy-start.1 = (f32[1,4608]{1,0:T(1,128)S(1)}, f32[1,4608]{1,0:T(1,128)}, u32[]{:S(2)}) copy-start(f32[1,4608]{1,0:T(1,128)} %first_ref.1) | copy-start | bytes 55300
  0.7 60.4 %copy-start = (f32[1,4608]{1,0:T(1,128)S(1)}, f32[1,4608]{1,0:T(1,128)}, u32[]{:S(2)}) copy-start(f32[1,4608]{1,0:T(1,128)} %master_ref.1) | copy-start | bytes 55300

commit v5 on v4

--- a/solution.py
+++ b/solution.py
@@ -237,7 +237,7 @@
 
     first_maxima = over_plane(m1_ref, r1_ref)
     ahead = 3
-    waves = [over_plane(bulk_ref.at[k], rbulk_ref.at[k]) for k in range(min(ahead, W))]
+    waves = [over_plane(bulk_ref.at[k], rbulk_ref.at[k]) for k in range(ahead - 1)]
     for k in range(W):
         rbulk_ref[k, here] = bulk_ref[k, y, x]
 
@@ -255,6 +255,7 @@
             adam_ref[i, k : k + 1, :] = state_ref[i, :, k * HAD : (k + 1) * HAD]
 
     landed(r1_ref, first_maxima)
+    waves.append(over_plane(bulk_ref.at[ahead - 1], rbulk_ref.at[ahead - 1]))
     peak = jnp.maximum(m1_ref[y, x], jnp.max(r1_ref[...], axis=0))
     m2_ref[...] = peak
     index = stage()
@@ -363,44 +364,59 @@
         ).start()
     sent.append((grad_ref.at[0 : NY - 1], column_sem))
 
-    groups = []
-    for j, o in enumerate(plane):
-        if j and plane_hops(NX, NY, plane[j - 1]) == plane_hops(NX, NY, o):
-            groups[-1][1] = j + 1
-        else:
-            groups.append([j, j + 1])
     core_sem = stage()
-
-    def share(part, rows_ref):
+    gathered = (gb_ref.at[c, 0], gb_ref.at[c, 1])
+
+    def pack(part, rows_ref):
         for k in range(W):
             both = jnp.concatenate([rows_ref[:, k, :], rows_ref[:, W + k, :]], axis=0)
-            gb_ref[c, part, here, :, k * LANES : (k + 1) * LANES] = both.astype(BF16)
+            gb_ref[c, part, 0, :, k * LANES : (k + 1) * LANES] = both.astype(BF16)
+
+    def along(part, axis, count):
+        slots_ref = gathered[part]
+        extent = (NX, NY)[axis]
         send = stage()
         recv = {}
-        for lo, hi in groups:
-            index = stage()
-            recv[lo] = index
-            for j in range(lo, hi):
-                copy(
-                    gb_ref.at[c, part, here], gb_ref.at[c, part, j], plane_peer[j], send, index
-                ).start()
-        sent.append((gb_ref.at[c, part, 0:here], send))
+        for o in sorted(range(1, extent), key=lambda o: -ring_distance(o, extent)):
+            recv[o] = stage()
+            peer = device(o, 0, 0, 0) if axis == 0 else device(0, o, 0, 0)
+            copy(
+                slots_ref.at[0:count],
+                slots_ref.at[count * o : count * (o + 1)],
+                peer,
+                send,
+                recv[o],
+            ).start()
+        sent.append((slots_ref.at[count : count * extent], send))
         return recv
 
-    def pass_on(part, recv):
-        for lo, hi in reversed(groups):
-            landed(gb_ref.at[c, part, lo:hi], recv[lo])
-            hi = here + 1 if hi == here else hi
-            piece = gb_ref.at[c, part, lo:hi]
-            copy(piece, piece, core_peer, core_sem, core_sem).start()
+    def arrive(part, recv, count, forward):
+        slots_ref = gathered[part]
+        for o in sorted(recv, key=lambda o: ring_distance(o, len(recv) + 1)):
+            piece = slots_ref.at[count * o : count * (o + 1)]
+            landed(piece, recv[o])
+            if forward:
+                copy(piece, piece, core_peer, core_sem, core_sem).start()
+
+    def pass_on(part, count):
+        piece = gathered[part].at[0:count]
+        copy(piece, piece, core_peer, core_sem, core_sem).start()
 
     if near:
         landed(near_ref.at[0 : len(near)], near_sem)
-    recv_near = share(0, near_ref)
+    pack(0, near_ref)
+    near_x = along(0, 0, 1)
     landed(far_ref, far_sem)
-    recv_far = share(1, far_ref)
-    pass_on(0, recv_near)
-    pass_on(1, recv_far)
+    pack(1, far_ref)
+    far_y = along(1, 1, 1)
+    arrive(0, near_x, 1, False)
+    near_y = along(0, 1, NX)
+    pass_on(0, NX)
+    arrive(1, far_y, 1, False)
+    far_x = along(1, 0, NY)
+    pass_on(1, NY)
+    arrive(0, near_y, NX, True)
+    arrive(1, far_x, NY, True)
     landed(grad_ref.at[0 : NY - 1], column_sem)
     landed(gb_ref.at[1 - c], core_sem)
     sent.append((gb_ref.at[c], core_sem))
@@ -424,8 +440,6 @@
 ):
     NX, NY, NZ, NB, W = sizes
     rows = NX * NZ * CORES
-    plane = plane_offsets(NX, NY)
-    slot_of = {o: j for j, o in enumerate(plane + [(0, 0)])}
     near, far = line_offsets(NZ)
     dp = lax.axis_index("dp")
     y = lax.axis_index("outer")
@@ -446,35 +460,36 @@
             for ref, value in zip((new_master_ref, new_first_ref, new_second_ref), results):
                 ref[0:1, lo : lo + HAD] = value[k : k + 1, :]
 
-    slots = CORES * 2 * NX * NZ
+    slots = rows
+    deep = NZ // 2
     r_at = lax.broadcasted_iota(jnp.int32, (rows, slots), 0)
     g_at = lax.broadcasted_iota(jnp.int32, (1, slots), 1)
-    low = lax.rem(g_at, NZ // 2)
-    second_half = lax.rem(g_at // (NZ // 2), 2)
-    ox = lax.rem(g_at // NZ, NX)
-    part = lax.rem(g_at // (NZ * NX), 2)
-    core = g_at // (NZ * NX * 2)
+    low = lax.rem(g_at, deep)
+    ox = lax.rem(g_at // deep, NX)
+    part = lax.rem(g_at // (deep * NX), 2)
+    core = g_at // (deep * NX * 2)
     back = max(NZ // 4 - 1, 0)
     near_o = jnp.where(low == len(near), 0, low - back + (low >= back).astype(jnp.int32))
     oz = jnp.where(part == 0, near_o, low + NZ // 2 - back)
     source = (lax.rem(x - ox + NX, NX) * NZ + lax.rem(z - oz + NZ, NZ)) * CORES + core
-    pick = [
-        (r_at == jnp.where(second_half == h, source, -1)).astype(F32).astype(BF16)
-        for h in range(2)
-    ]
+    pick = (r_at == source).astype(F32).astype(BF16)
     for oy in range(NY):
         at = lax.rem(y + NY - oy, NY)
         begin = piece_start(sizes, at) * HAD
-        value = jnp.concatenate(
-            [
-                gb_ref[core, part, slot_of[(ox, oy)]]
-                for core in range(CORES)
-                for part in range(2)
-                for ox in range(NX)
-            ],
-            axis=0,
-        )
-        tiles = [dot(pick[h], value).astype(BF16) for h in range(2)]
+        tiles = []
+        for h in range(2):
+            value = jnp.concatenate(
+                [
+                    gb_ref[
+                        core, part, ox * NY + oy if part else oy * NX + ox, h * deep : (h + 1) * deep
+                    ]
+                    for core in range(CORES)
+                    for part in range(2)
+                    for ox in range(NX)
+                ],
+                axis=0,
+            )
+            tiles.append(dot(pick, value).astype(BF16))
         for k in range(W):
             both = jnp.concatenate(
                 [tile[:, k * LANES : (k + 1) * LANES] for tile in tiles], axis=1
@@ -497,8 +512,7 @@
     pair = CORES * NZ
     n_plane = NX * NY - 1
     n_line = NZ - 1
-    groups = len({plane_hops(NX, NY, o) for o in plane_offsets(NX, NY)})
-    stages = 10 + 2 * W + 2 * (groups + 1)
+    stages = 10 + 2 * W + 2 * (NX + NY)
     near, far = line_offsets(NZ)
     width = NB * HAD
     piece = W * HAD

time: 63.4 us -> 64 us (level)
    pallas_call x1, Pallas kernels: 60.3 us -> 61 us  [per_device(): pl.pallas_call(functools.partial(exchange_kernel, sizes), out_shape=(pltp...]
where the time goes in v5:
time: 64 us; the launch traced here: 63.8 us
  Pallas kernels  63.1 us (99%)
  between operations  0.69 us (1%)
    pallas_call x1, Pallas kernels, per_device(): pl.pallas_call(functools.partial(exchange_kernel, sizes), out_shape=(pltp...  61 us
    pallas_call x1, Pallas kernels, per_device(): pl.pallas_call(functools.partial(write_kernel, sizes), out_shape=(row, ro...  2.08 us

profile of v5, /device:TPU:1, one launch (start us, length us, event | category | flops | bytes accessed | tf_op | source)
XLA Modules:
  0.0 63.8 jit_solution(4738393254250064460)
XLA Ops:
  0.6 0.0 copy-start.2
  0.6 0.0 copy-start.1
  0.7 0.0 copy-start
  0.7 61.0 %shard_map.84 = (bf16[2,2,16,16,640]{4,3,2,1,0:T(8,128)(2,1)S(1)}, f32[4,5,256]{2,1,0:T(8,128)S(1)}) custom-call(bf16[1,1,128,4608]{3,2,1,0:T(8,128)(2,1)} %grads_hbm.1, s32[1,256]{1,0:T(1,128)} %bitcast.1, f32[1,4608]{1,0:T(1,128)} %master_ref.1, f32[1,4608]{1,0:T(1,128)} %first_ref.1, f32[1,4608]{1,0:T(1,128)} %second_ref.1), custom_call_target="tpu_custom_call" | custom-call | tf_op jit(solution)/shard_map/pallas_call | solution.py:549
  61.7 0.0 copy-done.2
  61.7 0.0 copy-done.1
  61.7 0.0 copy-done
  61.7 2.1 %shard_map.85 = (f32[1,4608]{1,0:T(1,128)}, f32[1,4608]{1,0:T(1,128)}, f32[1,4608]{1,0:T(1,128)}, bf16[128,4608]{1,0:T(8,128)(2,1)}) custom-call(bf16[2,2,16,16,640]{4,3,2,1,0:T(8,128)(2,1)S(1)} %get-tuple-element.6.gb_ref, f32[4,5,256]{2,1,0:T(8,128)S(1)} %get-tuple-element.7.grad_ref, f32[1,4608]{1,0:T(1,128)S(1)} %copy-done, f32[1,4608]{1,0:T(1,128)S(1)} %copy-done.1, ...), custom_call_target="tpu_custom_call" | custom-call | tf_op jit(solution)/shard_map/pallas_call | solution.py:573
Async XLA Ops:
  0.6 61.0 %copy-start.2 = (f32[1,4608]{1,0:T(1,128)S(1)}, f32[1,4608]{1,0:T(1,128)}, u32[]{:S(2)}) copy-start(f32[1,4608]{1,0:T(1,128)} %second_ref.1) | copy-start | bytes 55300
  0.6 61.0 %copy-start.1 = (f32[1,4608]{1,0:T(1,128)S(1)}, f32[1,4608]{1,0:T(1,128)}, u32[]{:S(2)}) copy-start(f32[1,4608]{1,0:T(1,128)} %first_ref.1) | copy-start | bytes 55300
  0.7 61.0 %copy-start = (f32[1,4608]{1,0:T(1,128)S(1)}, f32[1,4608]{1,0:T(1,128)}, u32[]{:S(2)}) copy-start(f32[1,4608]{1,0:T(1,128)} %master_ref.1) | copy-start | bytes 55300

commit v6 on v5

--- a/solution.py
+++ b/solution.py
@@ -90,6 +90,7 @@
     master_hbm,
     first_hbm,
     second_hbm,
+    ga_ref,
     gb_ref,
     grad_ref,
     x_ref,
@@ -364,17 +365,22 @@
         ).start()
     sent.append((grad_ref.at[0 : NY - 1], column_sem))
 
-    core_sem = stage()
-    gathered = (gb_ref.at[c, 0], gb_ref.at[c, 1])
-
-    def pack(part, rows_ref):
+    WA = W // 2
+    core_sems = (stage(), stage())
+    sets = (ga_ref, gb_ref)
+    extents = (NX, NY)
+
+    def pack(wave, rows_ref):
         for k in range(W):
             both = jnp.concatenate([rows_ref[:, k, :], rows_ref[:, W + k, :]], axis=0)
-            gb_ref[c, part, 0, :, k * LANES : (k + 1) * LANES] = both.astype(BF16)
-
-    def along(part, axis, count):
-        slots_ref = gathered[part]
-        extent = (NX, NY)[axis]
+            at = k if k < WA else k - WA
+            sets[int(k >= WA)][c, wave, 0, :, at * LANES : (at + 1) * LANES] = both.astype(BF16)
+
+    def along(wave, which, step):
+        slots_ref = sets[which].at[c, wave]
+        axis = which ^ step
+        count = extents[which] if step else 1
+        extent = extents[axis]
         send = stage()
         recv = {}
         for o in sorted(range(1, extent), key=lambda o: -ring_distance(o, extent)):
@@ -390,36 +396,45 @@
         sent.append((slots_ref.at[count : count * extent], send))
         return recv
 
-    def arrive(part, recv, count, forward):
-        slots_ref = gathered[part]
+    def arrive(wave, which, step, recv):
+        slots_ref = sets[which].at[c, wave]
+        count = extents[which] if step else 1
         for o in sorted(recv, key=lambda o: ring_distance(o, len(recv) + 1)):
             piece = slots_ref.at[count * o : count * (o + 1)]
             landed(piece, recv[o])
-            if forward:
-                copy(piece, piece, core_peer, core_sem, core_sem).start()
-
-    def pass_on(part, count):
-        piece = gathered[part].at[0:count]
-        copy(piece, piece, core_peer, core_sem, core_sem).start()
+            if step:
+                copy(piece, piece, core_peer, core_sems[which], core_sems[which]).start()
+
+    def pass_on(wave, which):
+        piece = sets[which].at[c, wave, 0 : extents[which]]
+        copy(piece, piece, core_peer, core_sems[which], core_sems[which]).start()
 
     if near:
         landed(near_ref.at[0 : len(near)], near_sem)
     pack(0, near_ref)
-    near_x = along(0, 0, 1)
+    near_one = [along(0, which, 0) for which in range(2)]
     landed(far_ref, far_sem)
     pack(1, far_ref)
-    far_y = along(1, 1, 1)
-    arrive(0, near_x, 1, False)
-    near_y = along(0, 1, NX)
-    pass_on(0, NX)
-    arrive(1, far_y, 1, False)
-    far_x = along(1, 0, NY)
-    pass_on(1, NY)
-    arrive(0, near_y, NX, True)
-    arrive(1, far_x, NY, True)
+    far_one = [along(1, which, 0) for which in range(2)]
+    near_two = []
+    far_two = []
+    for which in range(2):
+        arrive(0, which, 0, near_one[which])
+        near_two.append(along(0, which, 1))
+    for which in range(2):
+        arrive(1, which, 0, far_one[which])
+        far_two.append(along(1, which, 1))
+    for wave in range(2):
+        for which in range(2):
+            pass_on(wave, which)
+    for which in range(2):
+        arrive(0, which, 1, near_two[which])
+    for which in range(2):
+        arrive(1, which, 1, far_two[which])
     landed(grad_ref.at[0 : NY - 1], column_sem)
-    landed(gb_ref.at[1 - c], core_sem)
-    sent.append((gb_ref.at[c], core_sem))
+    for which in range(2):
+        landed(sets[which].at[1 - c], core_sems[which])
+        sent.append((sets[which].at[c], core_sems[which]))
 
     for ref, index in sent:
         copy(ref, ref, core_peer, index, index).wait_send()
@@ -427,6 +442,7 @@
 
 def write_kernel(
     sizes,
+    ga_ref,
     gb_ref,
     grad_ref,
     master_ref,
@@ -478,18 +494,24 @@
         begin = piece_start(sizes, at) * HAD
         tiles = []
         for h in range(2):
-            value = jnp.concatenate(
-                [
-                    gb_ref[
-                        core, part, ox * NY + oy if part else oy * NX + ox, h * deep : (h + 1) * deep
-                    ]
-                    for core in range(CORES)
-                    for part in range(2)
-                    for ox in range(NX)
-                ],
-                axis=0,
-            )
-            tiles.append(dot(pick, value).astype(BF16))
+            parts = []
+            for which, ref in enumerate((ga_ref, gb_ref)):
+                value = jnp.concatenate(
+                    [
+                        ref[
+                            core,
+                            wave,
+                            ox * NY + oy if which else oy * NX + ox,
+                            h * deep : (h + 1) * deep,
+                        ]
+                        for core in range(CORES)
+                        for wave in range(2)
+                        for ox in range(NX)
+                    ],
+                    axis=0,
+                )
+                parts.append(dot(pick, value).astype(BF16))
+            tiles.append(jnp.concatenate(parts, axis=1))
         for k in range(W):
             both = jnp.concatenate(
                 [tile[:, k * LANES : (k + 1) * LANES] for tile in tiles], axis=1
@@ -512,7 +534,8 @@
     pair = CORES * NZ
     n_plane = NX * NY - 1
     n_line = NZ - 1
-    stages = 10 + 2 * W + 2 * (NX + NY)
+    stages = 11 + 2 * W + 4 * (NX + NY)
+    set_a = (W // 2) * LANES
     near, far = line_offsets(NZ)
     width = NB * HAD
     piece = W * HAD
@@ -546,14 +569,15 @@
     row = jax.ShapeDtypeStruct((1, width), F32)
 
     def per_device(replica_grads, hadamard_signs, master_rows, first_moment, second_moment):
-        gathered, gradients = pl.pallas_call(
+        first_set, second_set, gradients = pl.pallas_call(
             functools.partial(exchange_kernel, sizes),
             out_shape=(
-                pltpu.VMEM((CORES, 2, n_plane + 1, NZ, piece // 2), BF16),
+                pltpu.VMEM((CORES, 2, n_plane + 1, NZ, set_a), BF16),
+                pltpu.VMEM((CORES, 2, n_plane + 1, NZ, piece // 2 - set_a), BF16),
                 pltpu.VMEM((NY, W, HAD), F32),
             ),
             in_specs=[pl.BlockSpec(memory_space=pltpu.HBM)] * 5,
-            out_specs=(vmem, vmem),
+            out_specs=(vmem, vmem, vmem),
             scratch_shapes=scratch,
             compiler_params=pltpu.CompilerParams(
                 collective_id=0, has_side_effects=True, vmem_limit_bytes=40 * 2**20
@@ -573,11 +597,11 @@
         return pl.pallas_call(
             functools.partial(write_kernel, sizes),
             out_shape=(row, row, row, jax.ShapeDtypeStruct((rows, width), BF16)),
-            in_specs=[vmem] * 5,
+            in_specs=[vmem] * 6,
             out_specs=(vmem,) * 4,
             scratch_shapes=[pltpu.VMEM((3, W, HAD), F32)],
             compiler_params=pltpu.CompilerParams(vmem_limit_bytes=20 * 2**20),
-        )(gathered, gradients, master_rows, first_moment, second_moment)
+        )(first_set, second_set, gradients, master_rows, first_moment, second_moment)
 
     in_specs = (P("dp", "outer", None, None), P(), P("dp", None), P("dp", None), P("dp", None))
     out_specs = (P("dp", None), P("dp", None), P("dp", None), P())

time: 64 us -> 63.4 us (level)
  no operation moved by 1% of the time
where the time goes in v6:
time: 63.4 us; the launch traced here: 63.3 us
  Pallas kernels  62.6 us (99%)
  between operations  0.69 us (1%)
    pallas_call x1, Pallas kernels, per_device(): pl.pallas_call(functools.partial(exchange_kernel, sizes), out_shape=(pltp...  60.5 us
    pallas_call x1, Pallas kernels, per_device(): pl.pallas_call(functools.partial(write_kernel, sizes), out_shape=(row, ro...  2.07 us

profile of v6, /device:TPU:1, one launch (start us, length us, event | category | flops | bytes accessed | tf_op | source)
XLA Modules:
  0.0 63.3 jit_solution(7324457403146439594)
XLA Ops:
  0.6 0.0 copy-start.2
  0.6 0.0 copy-start.1
  0.7 0.0 copy-start
  0.7 60.5 %shard_map.84 = (bf16[2,2,16,16,256]{4,3,2,1,0:T(8,128)(2,1)S(1)}, bf16[2,2,16,16,384]{4,3,2,1,0:T(8,128)(2,1)S(1)}, f32[4,5,256]{2,1,0:T(8,128)S(1)}) custom-call(bf16[1,1,128,4608]{3,2,1,0:T(8,128)(2,1)} %grads_hbm.1, s32[1,256]{1,0:T(1,128)} %bitcast.1, f32[1,4608]{1,0:T(1,128)} %master_ref.1, f32[1,4608]{1,0:T(1,128)} %first_ref.1, f32[1,4608]{1,0:T(1,128)} %second_ref.1), custom_call_target="tpu_custom_call" | custom-call | tf_op jit(solution)/shard_map/pallas_call | solution.py:572
  61.1 0.0 copy-done.2
  61.2 0.0 copy-done.1
  61.2 0.0 copy-done
  61.2 2.1 %shard_map.85 = (f32[1,4608]{1,0:T(1,128)}, f32[1,4608]{1,0:T(1,128)}, f32[1,4608]{1,0:T(1,128)}, bf16[128,4608]{1,0:T(8,128)(2,1)}) custom-call(bf16[2,2,16,16,256]{4,3,2,1,0:T(8,128)(2,1)S(1)} %get-tuple-element.7.ga_ref, bf16[2,2,16,16,384]{4,3,2,1,0:T(8,128)(2,1)S(1)} %get-tuple-element.8.gb_ref, f32[4,5,256]{2,1,0:T(8,128)S(1)} %get-tuple-element.9.grad_ref, ...), custom_call_target="tpu_custom_call" | custom-call | tf_op jit(solution)/shard_map/pallas_call | solution.py:597
Async XLA Ops:
  0.6 60.5 %copy-start.2 = (f32[1,4608]{1,0:T(1,128)S(1)}, f32[1,4608]{1,0:T(1,128)}, u32[]{:S(2)}) copy-start(f32[1,4608]{1,0:T(1,128)} %second_ref.1) | copy-start | bytes 55300
  0.6 60.5 %copy-start.1 = (f32[1,4608]{1,0:T(1,128)S(1)}, f32[1,4608]{1,0:T(1,128)}, u32[]{:S(2)}) copy-start(f32[1,4608]{1,0:T(1,128)} %first_ref.1) | copy-start | bytes 55300
  0.7 60.5 %copy-start = (f32[1,4608]{1,0:T(1,128)S(1)}, f32[1,4608]{1,0:T(1,128)}, u32[]{:S(2)}) copy-start(f32[1,4608]{1,0:T(1,128)} %master_ref.1) | copy-start | bytes 55300

commit v7 on v6

--- a/solution.py
+++ b/solution.py
@@ -148,16 +148,15 @@
     line_peer = {o: device(0, 0, o, 0) for o in line}
     here = len(plane)
 
+    grads_load = pltpu.make_async_copy(grads_hbm.at[0, 0], x_ref, load_sems.at[0])
+    grads_load.start()
     barrier = pltpu.get_barrier_semaphore()
     peers = [line_peer[o] for o in line] + plane_peer + [core_peer]
     for peer in peers:
         pl.semaphore_signal(barrier, inc=1, device_id=peer, device_id_type=MESH)
 
     begin = pl.multiple_of(first_block(y) * HAD, HAD)
-    loads = [
-        pltpu.make_async_copy(grads_hbm.at[0, 0], x_ref, load_sems.at[0]),
-        pltpu.make_async_copy(signs_hbm, signs_ref, load_sems.at[1]),
-    ]
+    loads = [pltpu.make_async_copy(signs_hbm, signs_ref, load_sems.at[1])]
     for i, hbm in enumerate((master_hbm, first_hbm, second_hbm)):
         loads.append(
             pltpu.make_async_copy(
@@ -167,7 +166,7 @@
     for load in loads:
         load.start()
 
-    counter = [0]
+    counter = {True: 0, False: 0}
     sent = []
 
     def copy(src, dst, peer, send, recv):
@@ -180,12 +179,12 @@
             device_id_type=MESH,
         )
 
-    def stage():
-        counter[0] += 1
-        return counter[0] - 1
+    def stage(send):
+        counter[send] += 1
+        return counter[send] - 1
 
     def landed(ref, index):
-        copy(ref, ref, core_peer, index, index).wait_recv()
+        copy(ref, ref, core_peer, 0, index).wait_recv()
 
     p_at = lax.broadcasted_iota(jnp.int32, (rows, rows), 0)
     r_at = lax.broadcasted_iota(jnp.int32, (1, rows), 1)
@@ -197,7 +196,7 @@
     table = hadamard(BF16)
     table_ref[...] = table
 
-    loads[0].wait()
+    grads_load.wait()
 
     lane = lax.rem(lax.broadcasted_iota(jnp.int32, (1, LANES), 1), stride)
     picks = [
@@ -228,24 +227,26 @@
 
     pl.semaphore_wait(barrier, len(peers))
 
-    def over_plane(parts_ref, slots_ref):
-        index = stage()
+    def over_plane(parts_ref, slots_ref, send):
+        recv = stage(False)
         for j, o in enumerate(plane):
             piece = parts_ref.at[lax.rem(y + o[1], NY), lax.rem(x + o[0], NX)]
-            copy(piece, slots_ref.at[j], plane_peer[j], index, index).start()
-        sent.append((slots_ref.at[0:here], index))
-        return index
-
-    first_maxima = over_plane(m1_ref, r1_ref)
+            copy(piece, slots_ref.at[j], plane_peer[j], send, recv).start()
+        return recv
+
+    maxima_send = stage(True)
+    first_maxima = over_plane(m1_ref, r1_ref, maxima_send)
+    sent.append((r1_ref, maxima_send))
+    bulk_send = stage(True)
     ahead = 3
-    waves = [over_plane(bulk_ref.at[k], rbulk_ref.at[k]) for k in range(ahead - 1)]
+    waves = [over_plane(bulk_ref.at[k], rbulk_ref.at[k], bulk_send) for k in range(ahead - 1)]
     for k in range(W):
         rbulk_ref[k, here] = bulk_ref[k, y, x]
 
     diagonal = lax.broadcasted_iota(jnp.int32, (HAD, HAD), 0) == lax.broadcasted_iota(
         jnp.int32, (HAD, HAD), 1
     )
-    for load in loads[1:]:
+    for load in loads:
         load.wait()
     sign_row = signs_ref[...].astype(F32)
     signed_ref[...] = dot(
@@ -256,28 +257,29 @@
             adam_ref[i, k : k + 1, :] = state_ref[i, :, k * HAD : (k + 1) * HAD]
 
     landed(r1_ref, first_maxima)
-    waves.append(over_plane(bulk_ref.at[ahead - 1], rbulk_ref.at[ahead - 1]))
+    waves.append(over_plane(bulk_ref.at[ahead - 1], rbulk_ref.at[ahead - 1], bulk_send))
     peak = jnp.maximum(m1_ref[y, x], jnp.max(r1_ref[...], axis=0))
     m2_ref[...] = peak
-    index = stage()
-    copy(m2_ref, r2_ref, core_peer, index, index).start()
-    sent.append((r2_ref, index))
-    landed(r2_ref, index)
+    send, recv = stage(True), stage(False)
+    copy(m2_ref, r2_ref, core_peer, send, recv).start()
+    sent.append((r2_ref, send))
+    landed(r2_ref, recv)
     peak = jnp.maximum(peak, r2_ref[...])
     m3_ref[...] = peak
-    last_maxima = stage()
+    send, last_maxima = stage(True), stage(False)
     for j, o in enumerate(line):
-        copy(m3_ref, r3_ref.at[j], line_peer[o], last_maxima, last_maxima).start()
-    sent.append((r3_ref, last_maxima))
+        copy(m3_ref, r3_ref.at[j], line_peer[o], send, last_maxima).start()
+    sent.append((r3_ref, send))
 
     signed = signed_ref[...]
     for k in range(W):
         landed(rbulk_ref.at[k, 0:here], waves[k])
         if k + ahead < W:
-            waves.append(over_plane(bulk_ref.at[k + ahead], rbulk_ref.at[k + ahead]))
+            waves.append(over_plane(bulk_ref.at[k + ahead], rbulk_ref.at[k + ahead], bulk_send))
         value = rbulk_ref[k].reshape((here + 1) * pair, HAD)
         rot_ref[k] = dot(value, signed).reshape(here + 1, pair, HAD)
 
+    sent.append((rbulk_ref.at[:, 0:here], bulk_send))
     landed(r3_ref, last_maxima)
     peak = jnp.maximum(peak, jnp.max(r3_ref[...], axis=0))
 
@@ -285,8 +287,8 @@
     inverse = 0.0625 / scales
     z_at = lax.broadcasted_iota(jnp.int32, (NZ, LANES), 0)
     l_at = lax.broadcasted_iota(jnp.int32, (NZ, LANES), 1)
-    core_send = stage()
-    core_recv = [stage() for _ in range(W)]
+    core_send = stage(True)
+    core_recv = [stage(False) for _ in range(W)]
     for k in range(W):
         cols = slice(k * HAD, (k + 1) * HAD)
         pick = l_at == z_at * stride + k
@@ -326,14 +328,12 @@
             cols = slice(k * HAD + h * LANES, k * HAD + (h + 1) * LANES)
             zs_ref[:, h * W + k, :] = acc_ref[c, :, cols] + racc_ref[:, cols]
 
-    index = stage()
+    send, recv = stage(True), stage(False)
     for j, o in enumerate(line):
-        copy(
-            zs_ref.at[lax.rem(z + o, NZ)], rz_ref.at[j], line_peer[o], index, index
-        ).start()
-    sent.append((rz_ref, index))
+        copy(zs_ref.at[lax.rem(z + o, NZ)], rz_ref.at[j], line_peer[o], send, recv).start()
+    sent.append((rz_ref, send))
     own_part = zs_ref[z]
-    landed(rz_ref, index)
+    landed(rz_ref, recv)
     total = own_part + jnp.sum(rz_ref[...], axis=0)
 
     wide = jnp.concatenate([total[0:W], total[W : 2 * W]], axis=1)
@@ -347,26 +347,28 @@
     near_ref[len(near), 0:W] = updated[:, 0:LANES]
     near_ref[len(near), W : 2 * W] = updated[:, LANES:HAD]
 
-    far_sem = stage()
-    near_sem = stage()
+    far_send, far_recv = stage(True), stage(False)
+    near_send, near_recv = stage(True), stage(False)
     mine = near_ref.at[len(near)]
-    slots = {o % NZ: (near_ref.at[i], near_sem) for i, o in enumerate(near)}
-    slots.update({o % NZ: (far_ref.at[i], far_sem) for i, o in enumerate(far)})
+    slots = {o % NZ: (near_ref.at[i], near_send, near_recv) for i, o in enumerate(near)}
+    slots.update({o % NZ: (far_ref.at[i], far_send, far_recv) for i, o in enumerate(far)})
     for o in line:
-        slot, index = slots[o]
-        copy(mine, slot, line_peer[o], index, index).start()
-    sent.append((far_ref, far_sem))
+        slot, send, recv = slots[o]
+        copy(mine, slot, line_peer[o], send, recv).start()
+    sent.append((far_ref, far_send))
     if near:
-        sent.append((near_ref.at[0 : len(near)], near_sem))
-    column_sem = stage()
+        sent.append((near_ref.at[0 : len(near)], near_send))
+    column_send, column_recv = stage(True), stage(False)
     for o in column:
         copy(
-            grad_ref.at[y], grad_ref.at[y], device(0, o, 0, 0), column_sem, column_sem
+            grad_ref.at[y], grad_ref.at[y], device(0, o, 0, 0), column_send, column_recv
         ).start()
-    sent.append((grad_ref.at[0 : NY - 1], column_sem))
+    sent.append((grad_ref.at[0 : NY - 1], column_send))
 
     WA = W // 2
-    core_sems = (stage(), stage())
+    core_sends = (stage(True), stage(True))
+    core_recvs = (stage(False), stage(False))
+    step_sends = [[stage(True) for _ in range(2)] for _ in range(2)]
     sets = (ga_ref, gb_ref)
     extents = (NX, NY)
 
@@ -381,10 +383,11 @@
         axis = which ^ step
         count = extents[which] if step else 1
         extent = extents[axis]
-        send = stage()
+        send = step_sends[which][step]
+        first = stage(False)
         recv = {}
         for o in sorted(range(1, extent), key=lambda o: -ring_distance(o, extent)):
-            recv[o] = stage()
+            recv[o] = stage(False) if step and recv else first
             peer = device(o, 0, 0, 0) if axis == 0 else device(0, o, 0, 0)
             copy(
                 slots_ref.at[0:count],
@@ -393,27 +396,29 @@
                 send,
                 recv[o],
             ).start()
-        sent.append((slots_ref.at[count : count * extent], send))
+        if wave:
+            sent.append((sets[which].at[c, :, count : count * extent], send))
         return recv
+
+    def pass_on(which, piece):
+        copy(piece, piece, core_peer, core_sends[which], core_recvs[which]).start()
 
     def arrive(wave, which, step, recv):
         slots_ref = sets[which].at[c, wave]
-        count = extents[which] if step else 1
+        if step == 0:
+            landed(slots_ref.at[1 : len(recv) + 1], recv[1])
+            return
+        count = extents[which]
         for o in sorted(recv, key=lambda o: ring_distance(o, len(recv) + 1)):
             piece = slots_ref.at[count * o : count * (o + 1)]
             landed(piece, recv[o])
-            if step:
-                copy(piece, piece, core_peer, core_sems[which], core_sems[which]).start()
-
-    def pass_on(wave, which):
-        piece = sets[which].at[c, wave, 0 : extents[which]]
-        copy(piece, piece, core_peer, core_sems[which], core_sems[which]).start()
+            pass_on(which, piece)
 
     if near:
-        landed(near_ref.at[0 : len(near)], near_sem)
+        landed(near_ref.at[0 : len(near)], near_recv)
     pack(0, near_ref)
     near_one = [along(0, which, 0) for which in range(2)]
-    landed(far_ref, far_sem)
+    landed(far_ref, far_recv)
     pack(1, far_ref)
     far_one = [along(1, which, 0) for which in range(2)]
     near_two = []
@@ -426,18 +431,18 @@
         far_two.append(along(1, which, 1))
     for wave in range(2):
         for which in range(2):
-            pass_on(wave, which)
+            pass_on(which, sets[which].at[c, wave, 0 : extents[which]])
     for which in range(2):
         arrive(0, which, 1, near_two[which])
     for which in range(2):
         arrive(1, which, 1, far_two[which])
-    landed(grad_ref.at[0 : NY - 1], column_sem)
+    landed(grad_ref.at[0 : NY - 1], column_recv)
     for which in range(2):
-        landed(sets[which].at[1 - c], core_sems[which])
-        sent.append((sets[which].at[c], core_sems[which]))
+        landed(sets[which].at[1 - c], core_recvs[which])
+        sent.append((sets[which].at[c], core_sends[which]))
 
     for ref, index in sent:
-        copy(ref, ref, core_peer, index, index).wait_send()
+        copy(ref, ref, core_peer, index, 0).wait_send()
 
 
 def write_kernel(
@@ -451,8 +456,10 @@
     new_master_ref,
     new_first_ref,
     new_second_ref,
+    out_hbm,
+    adam_ref,
     out_ref,
-    adam_ref,
+    out_sems,
 ):
     NX, NY, NZ, NB, W = sizes
     rows = NX * NZ * CORES
@@ -461,20 +468,6 @@
     y = lax.axis_index("outer")
     z = lax.rem(dp // CORES, NZ)
     x = dp // (CORES * NZ)
-
-    for at in range(NY):
-        begin = piece_start(sizes, at)
-        for k in range(W):
-            lo = (begin + k) * HAD
-            adam_ref[0, k : k + 1, :] = master_ref[0:1, lo : lo + HAD]
-            adam_ref[1, k : k + 1, :] = first_ref[0:1, lo : lo + HAD]
-            adam_ref[2, k : k + 1, :] = second_ref[0:1, lo : lo + HAD]
-        results = adam(grad_ref[at], adam_ref[0], adam_ref[1], adam_ref[2])
-        end = piece_start(sizes, at + 1) if at < NY - 1 else NB
-        for k in range(end - begin):
-            lo = (begin + k) * HAD
-            for ref, value in zip((new_master_ref, new_first_ref, new_second_ref), results):
-                ref[0:1, lo : lo + HAD] = value[k : k + 1, :]
 
     slots = rows
     deep = NZ // 2
@@ -489,6 +482,8 @@
     oz = jnp.where(part == 0, near_o, low + NZ // 2 - back)
     source = (lax.rem(x - ox + NX, NX) * NZ + lax.rem(z - oz + NZ, NZ)) * CORES + core
     pick = (r_at == source).astype(F32).astype(BF16)
+    most = []
+    lasts = []
     for oy in range(NY):
         at = lax.rem(y + NY - oy, NY)
         begin = piece_start(sizes, at) * HAD
@@ -516,14 +511,43 @@
             both = jnp.concatenate(
                 [tile[:, k * LANES : (k + 1) * LANES] for tile in tiles], axis=1
             )
-            cols = pl.ds(pl.multiple_of(begin + k * HAD, HAD), HAD)
-            if k < W - 1:
-                out_ref[:, cols] = both
-            else:
-
-                @pl.when((at == 0) | (at == NY - 1))
-                def _():
-                    out_ref[:, cols] = both
+            out_ref[oy, :, k * HAD : (k + 1) * HAD] = both
+        kept = (W - 1) * HAD
+        cols = pl.ds(pl.multiple_of(begin, HAD), kept)
+        most.append(
+            pltpu.make_async_copy(out_ref.at[oy, :, 0:kept], out_hbm.at[:, cols], out_sems.at[0, oy])
+        )
+        most[oy].start()
+        cols = pl.ds(pl.multiple_of(begin + kept, HAD), HAD)
+        last = pltpu.make_async_copy(
+            out_ref.at[oy, :, kept : W * HAD], out_hbm.at[:, cols], out_sems.at[1, oy]
+        )
+        lasts.append(((at == 0) | (at == NY - 1), last))
+
+        @pl.when(lasts[oy][0])
+        def _():
+            lasts[oy][1].start()
+
+    for at in range(NY):
+        begin = piece_start(sizes, at)
+        for k in range(W):
+            lo = (begin + k) * HAD
+            adam_ref[0, k : k + 1, :] = master_ref[0:1, lo : lo + HAD]
+            adam_ref[1, k : k + 1, :] = first_ref[0:1, lo : lo + HAD]
+            adam_ref[2, k : k + 1, :] = second_ref[0:1, lo : lo + HAD]
+        results = adam(grad_ref[at], adam_ref[0], adam_ref[1], adam_ref[2])
+        end = piece_start(sizes, at + 1) if at < NY - 1 else NB
+        for k in range(end - begin):
+            lo = (begin + k) * HAD
+            for ref, value in zip((new_master_ref, new_first_ref, new_second_ref), results):
+                ref[0:1, lo : lo + HAD] = value[k : k + 1, :]
+
+    for oy in range(NY):
+        most[oy].wait()
+
+        @pl.when(lasts[oy][0])
+        def _():
+            lasts[oy][1].wait()
 
 
 def build(mesh, NX, NZ, NB):
@@ -534,7 +558,8 @@
     pair = CORES * NZ
     n_plane = NX * NY - 1
     n_line = NZ - 1
-    stages = 11 + 2 * W + 4 * (NX + NY)
+    sends = 15
+    recvs = 10 + 2 * W + 4 + 2 * (NX + NY - 2)
     set_a = (W // 2) * LANES
     near, far = line_offsets(NZ)
     width = NB * HAD
@@ -562,8 +587,8 @@
         pltpu.VMEM((len(near) + 1, 2 * W, LANES), F32),
         pltpu.VMEM((len(far), 2 * W, LANES), F32),
         pltpu.SemaphoreType.DMA((5,)),
-        pltpu.SemaphoreType.DMA((stages,)),
-        pltpu.SemaphoreType.DMA((stages,)),
+        pltpu.SemaphoreType.DMA((sends,)),
+        pltpu.SemaphoreType.DMA((recvs,)),
     ]
     vmem = pl.BlockSpec(memory_space=pltpu.VMEM)
     row = jax.ShapeDtypeStruct((1, width), F32)
@@ -598,8 +623,12 @@
             functools.partial(write_kernel, sizes),
             out_shape=(row, row, row, jax.ShapeDtypeStruct((rows, width), BF16)),
             in_specs=[vmem] * 6,
-            out_specs=(vmem,) * 4,
-            scratch_shapes=[pltpu.VMEM((3, W, HAD), F32)],
+            out_specs=(vmem,) * 3 + (pl.BlockSpec(memory_space=pl.ANY),),
+            scratch_shapes=[
+                pltpu.VMEM((3, W, HAD), F32),
+                pltpu.VMEM((NY, rows, piece), BF16),
+                pltpu.SemaphoreType.DMA((2, NY)),
+            ],
             compiler_params=pltpu.CompilerParams(vmem_limit_bytes=20 * 2**20),
         )(first_set, second_set, gradients, master_rows, first_moment, second_moment)
 

time: 63.4 us -> 62.8 us (level)
  no operation moved by 1% of the time
where the time goes in v7:
time: 62.8 us; the launch traced here: 62.7 us
  Pallas kernels  62 us (99%)
  between operations  0.69 us (1%)
    pallas_call x1, Pallas kernels, per_device(): pl.pallas_call(functools.partial(exchange_kernel, sizes), out_shape=(pltp...  60 us
    pallas_call x1, Pallas kernels, per_device(): pl.pallas_call(functools.partial(write_kernel, sizes), out_shape=(row, ro...  2 us

profile of v7, /device:TPU:1, one launch (start us, length us, event | category | flops | bytes accessed | tf_op | source)
XLA Modules:
  0.0 62.7 jit_solution(13253100942171399923)
XLA Ops:
  0.6 0.0 copy-start.2
  0.6 0.0 copy-start.1
  0.7 0.0 copy-start
  0.7 60.0 %shard_map.84 = (bf16[2,2,16,16,256]{4,3,2,1,0:T(8,128)(2,1)S(1)}, bf16[2,2,16,16,384]{4,3,2,1,0:T(8,128)(2,1)S(1)}, f32[4,5,256]{2,1,0:T(8,128)S(1)}) custom-call(bf16[1,1,128,4608]{3,2,1,0:T(8,128)(2,1)} %grads_hbm.1, s32[1,256]{1,0:T(1,128)} %bitcast.1, f32[1,4608]{1,0:T(1,128)} %master_ref.1, f32[1,4608]{1,0:T(1,128)} %first_ref.1, f32[1,4608]{1,0:T(1,128)} %second_ref.1), custom_call_target="tpu_custom_call" | custom-call | tf_op jit(solution)/shard_map/pallas_call | solution.py:597
  60.6 0.0 copy-done.2
  60.6 0.0 copy-done.1
  60.6 0.0 copy-done
  60.7 2.0 %shard_map.85 = (f32[1,4608]{1,0:T(1,128)}, f32[1,4608]{1,0:T(1,128)}, f32[1,4608]{1,0:T(1,128)}, bf16[128,4608]{1,0:T(8,128)(2,1)}) custom-call(bf16[2,2,16,16,256]{4,3,2,1,0:T(8,128)(2,1)S(1)} %get-tuple-element.7.ga_ref, bf16[2,2,16,16,384]{4,3,2,1,0:T(8,128)(2,1)S(1)} %get-tuple-element.8.gb_ref, f32[4,5,256]{2,1,0:T(8,128)S(1)} %get-tuple-element.9.grad_ref, ...), custom_call_target="tpu_custom_call" | custom-call | tf_op jit(solution)/shard_map/pallas_call | solution.py:622
Async XLA Ops:
  0.6 60.0 %copy-start.2 = (f32[1,4608]{1,0:T(1,128)S(1)}, f32[1,4608]{1,0:T(1,128)}, u32[]{:S(2)}) copy-start(f32[1,4608]{1,0:T(1,128)} %second_ref.1) | copy-start | bytes 55300
  0.6 60.0 %copy-start.1 = (f32[1,4608]{1,0:T(1,128)S(1)}, f32[1,4608]{1,0:T(1,128)}, u32[]{:S(2)}) copy-start(f32[1,4608]{1,0:T(1,128)} %first_ref.1) | copy-start | bytes 55300
  0.7 60.0 %copy-start = (f32[1,4608]{1,0:T(1,128)S(1)}, f32[1,4608]{1,0:T(1,128)}, u32[]{:S(2)}) copy-start(f32[1,4608]{1,0:T(1,128)} %master_ref.1) | copy-start | bytes 55300

commit v8 on v7

--- a/solution.py
+++ b/solution.py
@@ -227,19 +227,34 @@
 
     pl.semaphore_wait(barrier, len(peers))
 
-    def over_plane(parts_ref, slots_ref, send):
+    def outer_piece(at):
+        return (at == 0) | (at == NY - 1)
+
+    def over_plane(parts_ref, slots_ref, send, outer_only=False):
         recv = stage(False)
         for j, o in enumerate(plane):
-            piece = parts_ref.at[lax.rem(y + o[1], NY), lax.rem(x + o[0], NX)]
-            copy(piece, slots_ref.at[j], plane_peer[j], send, recv).start()
+            at = lax.rem(y + o[1], NY)
+            piece = parts_ref.at[at, lax.rem(x + o[0], NX)]
+            message = copy(piece, slots_ref.at[j], plane_peer[j], send, recv)
+            if outer_only:
+                pl.when(outer_piece(at))(message.start)
+            else:
+                message.start()
         return recv
+
+    def send_block(k):
+        last = k == W - 1
+        send = last_send if last else bulk_send
+        waves.append(over_plane(bulk_ref.at[k], rbulk_ref.at[k], send, last))
 
     maxima_send = stage(True)
     first_maxima = over_plane(m1_ref, r1_ref, maxima_send)
     sent.append((r1_ref, maxima_send))
-    bulk_send = stage(True)
+    bulk_send, last_send = stage(True), stage(True)
     ahead = 3
-    waves = [over_plane(bulk_ref.at[k], rbulk_ref.at[k], bulk_send) for k in range(ahead - 1)]
+    waves = []
+    for k in range(ahead - 1):
+        send_block(k)
     for k in range(W):
         rbulk_ref[k, here] = bulk_ref[k, y, x]
 
@@ -257,7 +272,7 @@
             adam_ref[i, k : k + 1, :] = state_ref[i, :, k * HAD : (k + 1) * HAD]
 
     landed(r1_ref, first_maxima)
-    waves.append(over_plane(bulk_ref.at[ahead - 1], rbulk_ref.at[ahead - 1], bulk_send))
+    send_block(ahead - 1)
     peak = jnp.maximum(m1_ref[y, x], jnp.max(r1_ref[...], axis=0))
     m2_ref[...] = peak
     send, recv = stage(True), stage(False)
@@ -272,14 +287,28 @@
     sent.append((r3_ref, send))
 
     signed = signed_ref[...]
-    for k in range(W):
+    def rotate(k):
+        value = rbulk_ref[k].reshape((here + 1) * pair, HAD)
+        rot_ref[k] = dot(value, signed).reshape(here + 1, pair, HAD)
+
+    for k in range(W - 1):
         landed(rbulk_ref.at[k, 0:here], waves[k])
         if k + ahead < W:
-            waves.append(over_plane(bulk_ref.at[k + ahead], rbulk_ref.at[k + ahead], bulk_send))
-        value = rbulk_ref[k].reshape((here + 1) * pair, HAD)
-        rot_ref[k] = dot(value, signed).reshape(here + 1, pair, HAD)
-
-    sent.append((rbulk_ref.at[:, 0:here], bulk_send))
+            send_block(k + ahead)
+        rotate(k)
+
+    outer = outer_piece(y)
+
+    @pl.when(outer)
+    def _():
+        landed(rbulk_ref.at[W - 1, 0:here], waves[W - 1])
+        rotate(W - 1)
+
+    @pl.when(jnp.logical_not(outer))
+    def _():
+        rot_ref[W - 1] = jnp.zeros((here + 1, pair, HAD), F32)
+
+    sent.append((rbulk_ref.at[0 : W - 1, 0:here], bulk_send))
     landed(r3_ref, last_maxima)
     peak = jnp.maximum(peak, jnp.max(r3_ref[...], axis=0))
 
@@ -396,7 +425,7 @@
                 send,
                 recv[o],
             ).start()
-        if wave:
+        if wave and recv:
             sent.append((sets[which].at[c, :, count : count * extent], send))
         return recv
 
@@ -405,6 +434,8 @@
 
     def arrive(wave, which, step, recv):
         slots_ref = sets[which].at[c, wave]
+        if step == 0 and not recv:
+            return
         if step == 0:
             landed(slots_ref.at[1 : len(recv) + 1], recv[1])
             return
@@ -443,6 +474,13 @@
 
     for ref, index in sent:
         copy(ref, ref, core_peer, index, 0).wait_send()
+
+    def last_sent(count):
+        ref = rbulk_ref.at[W - 1, 0:count]
+        copy(ref, ref, core_peer, last_send, 0).wait_send()
+
+    pl.when(outer)(functools.partial(last_sent, 2 * NX - 1))
+    pl.when(jnp.logical_not(outer))(functools.partial(last_sent, 2 * NX))
 
 
 def write_kernel(
@@ -558,7 +596,7 @@
     pair = CORES * NZ
     n_plane = NX * NY - 1
     n_line = NZ - 1
-    sends = 15
+    sends = 16
     recvs = 10 + 2 * W + 4 + 2 * (NX + NY - 2)
     set_a = (W // 2) * LANES
     near, far = line_offsets(NZ)

time: 62.8 us -> 63.8 us (1.016)
  Pallas kernels: 62 us -> 62.9 us
    pallas_call x1, Pallas kernels: 60 us -> 60.9 us  [per_device(): pl.pallas_call(functools.partial(exchange_kernel, sizes), out_shape=(pltp...]
where the time goes in v8:
time: 63.8 us; the launch traced here: 63.6 us
  Pallas kernels  62.9 us (99%)
  between operations  0.69 us (1%)
    pallas_call x1, Pallas kernels, per_device(): pl.pallas_call(functools.partial(exchange_kernel, sizes), out_shape=(pltp...  60.9 us
    pallas_call x1, Pallas kernels, per_device(): pl.pallas_call(functools.partial(write_kernel, sizes), out_shape=(row, ro...  2 us

profile of v8, /device:TPU:1, one launch (start us, length us, event | category | flops | bytes accessed | tf_op | source)
XLA Modules:
  0.0 63.6 jit_solution(11167887506804243757)
XLA Ops:
  0.6 0.0 copy-start.2
  0.6 0.0 copy-start.1
  0.7 0.0 copy-start
  0.7 60.9 %shard_map.84 = (bf16[2,2,16,16,256]{4,3,2,1,0:T(8,128)(2,1)S(1)}, bf16[2,2,16,16,384]{4,3,2,1,0:T(8,128)(2,1)S(1)}, f32[4,5,256]{2,1,0:T(8,128)S(1)}) custom-call(bf16[1,1,128,4608]{3,2,1,0:T(8,128)(2,1)} %grads_hbm.1, s32[1,256]{1,0:T(1,128)} %bitcast.1, f32[1,4608]{1,0:T(1,128)} %master_ref.1, f32[1,4608]{1,0:T(1,128)} %first_ref.1, f32[1,4608]{1,0:T(1,128)} %second_ref.1), custom_call_target="tpu_custom_call" | custom-call | tf_op jit(solution)/shard_map/pallas_call | solution.py:635
  61.6 0.0 copy-done.2
  61.6 0.0 copy-done.1
  61.6 0.0 copy-done
  61.6 2.0 %shard_map.85 = (f32[1,4608]{1,0:T(1,128)}, f32[1,4608]{1,0:T(1,128)}, f32[1,4608]{1,0:T(1,128)}, bf16[128,4608]{1,0:T(8,128)(2,1)}) custom-call(bf16[2,2,16,16,256]{4,3,2,1,0:T(8,128)(2,1)S(1)} %get-tuple-element.7.ga_ref, bf16[2,2,16,16,384]{4,3,2,1,0:T(8,128)(2,1)S(1)} %get-tuple-element.8.gb_ref, f32[4,5,256]{2,1,0:T(8,128)S(1)} %get-tuple-element.9.grad_ref, ...), custom_call_target="tpu_custom_call" | custom-call | tf_op jit(solution)/shard_map/pallas_call | solution.py:660
Async XLA Ops:
  0.6 60.9 %copy-start.2 = (f32[1,4608]{1,0:T(1,128)S(1)}, f32[1,4608]{1,0:T(1,128)}, u32[]{:S(2)}) copy-start(f32[1,4608]{1,0:T(1,128)} %second_ref.1) | copy-start | bytes 55300
  0.6 60.9 %copy-start.1 = (f32[1,4608]{1,0:T(1,128)S(1)}, f32[1,4608]{1,0:T(1,128)}, u32[]{:S(2)}) copy-start(f32[1,4608]{1,0:T(1,128)} %first_ref.1) | copy-start | bytes 55300
  0.7 60.9 %copy-start = (f32[1,4608]{1,0:T(1,128)S(1)}, f32[1,4608]{1,0:T(1,128)}, u32[]{:S(2)}) copy-start(f32[1,4608]{1,0:T(1,128)} %master_ref.1) | copy-start | bytes 55300
